TPU v7x, 512 devices: a whole 4x4x16 slice. The times are simulated.
512 devices in a mesh: grp: 16 (over z_lo, core), lane: 32 (over z_hi, y, x).
Axes of the slice: x: 4, y: 4, z: 16 (z_hi: 2, z_lo: 8; z = z_hi * 8 + z_lo), core: 2. Of those that a mesh axis runs over, the one named last changes fastest.
Arguments:
- estimate: float32 [16, 1024, 1024], P('grp', 'lane'), may hold values from 0.5 to 2
- view_lines: float32 [4, 16384, 1024], P(None, ('grp', 'lane')), may hold values from 0.25 to 4
- line_owner: int32 [4, 16384, 1], P(None, ('grp', 'lane')), may hold values from 0 to 15; in each aligned block of 32 rows (0 to 31, 32 to 63, ..., all dimensions but the last counted through in order) at most 4 rows name the same one
- line_target: int32 [4, 16384], P(None, ('grp', 'lane')), may hold values from 0 to 31
- view_shift: int32 [4], replicated, may hold values from -16 to 16
- psf_x: float32 [4, 3], replicated, may hold values from 0.3 to 1
- psf_yz: float32 [4, 2, 41], replicated, may hold values from 0.001 to 1.5, as said below
Outputs:
- deconvolved: float32 [16, 1024, 1024], P('grp', 'lane')
Inputs may be any that keep to these rules, and one draw needn't show every extreme that they name: `line_owner`: for each view, among the 32 lines of one device no owner index appears more than 4 times, and some owner appears exactly 4 times in some of these blocks. `psf_yz`: positive tap weights.
All inputs are finite; a program needn't handle non-finite values.
Results may differ from a plain program's by a relative error of at most 0.0001.
Values sent between devices are 32-bit elements; how exact they have to be, the bound alone decides.
A program may use at most 128 MiB of HBM per device.

v0:
```python
import jax
import jax.numpy as jnp
from jax import lax
from jax.sharding import PartitionSpec as P

VIEWS = 4
ITERS = 2
SHIFT = 16


def with_halo(x, sides, width):
    for axis, dim in sides:
        devices, length = (lax.axis_size(axis), x.shape[dim])
        up = [(i, (i + 1) % devices) for i in range(devices - 1)]
        down = [(j, i) for i, j in up]
        last = lax.slice_in_dim(x, length - width, length, axis=dim)
        first = lax.slice_in_dim(x, 0, width, axis=dim)
        before = lax.ppermute(last, axis, up)
        after = lax.ppermute(first, axis, down)
        x = jnp.concatenate([before, x, after], axis=dim)
    return x


def shifted_sum(padded, kernel, stride, length, adjoint):
    extent = (kernel.shape[0] - 1) // 2
    summed = jnp.zeros(padded.shape[:-1] + (length,), jnp.float32)
    for position in range(kernel.shape[0]):
        offset = (position if adjoint else 2 * extent - position) * stride
        summed = summed + kernel[position] * lax.slice_in_dim(
            padded, offset, offset + length, axis=padded.ndim - 1
        )
    return summed


def spread_last(volume, kernel, stride, adjoint):
    extent = (kernel.shape[0] - 1) // 2
    pad_width = [(0, 0)] * (volume.ndim - 1) + [(extent * stride, extent * stride)]
    return shifted_sum(jnp.pad(volume, pad_width), kernel, stride, volume.shape[-1], adjoint)


def across_planes(volume, kernel, adjoint):
    planes, depth_dev, width_y = volume.shape
    extent = (kernel.shape[0] - 1) // 2
    widened = with_halo(volume, (("grp", 0),), extent)
    flattened = widened.reshape(1, -1)
    summed = shifted_sum(
        flattened, kernel, depth_dev * width_y, planes * depth_dev * width_y, adjoint
    )
    return summed.reshape(volume.shape)


def shift_line(line_rows, amount):
    return lax.dynamic_slice_in_dim(line_rows, SHIFT - amount, line_rows.shape[1] - 2 * SHIFT, 1)


def shards(estimate, view_lines, line_owner, line_target, view_shift, psf_x, psf_yz):
    planes, depth_dev, width_y = estimate.shape
    view_count, src_dev = line_target.shape
    groups = lax.axis_size("grp")
    capacity = 2 * src_dev // groups
    taps_x = psf_x / jnp.sum(psf_x, axis=1, keepdims=True)
    taps_yz = psf_yz / jnp.sum(psf_yz, axis=2, keepdims=True)
    padded = jnp.pad(view_lines, ((0, 0), (0, 0), (SHIFT, SHIFT)))
    shifted = jax.vmap(shift_line)(padded, view_shift)
    owners = line_owner[:, :, 0]
    onehot = (owners[:, :, None] == jnp.arange(groups, dtype=jnp.int32)[None, None, :]).astype(
        jnp.int32
    )
    slot_rank = jnp.sum(jnp.cumsum(onehot, axis=1) * onehot, axis=2) - 1
    slot_at = owners * capacity + slot_rank
    view_rows = jnp.arange(view_count, dtype=jnp.int32)[:, None]
    outgoing = (
        jnp.zeros((view_count, groups * capacity, width_y), jnp.float32)
        .at[view_rows, slot_at]
        .set(shifted)
    )
    targets = (
        jnp.full((view_count, groups * capacity), -1, jnp.int32)
        .at[view_rows, slot_at]
        .set(line_target)
    )
    arrived, arrived_at = (
        lax.all_to_all(outgoing, "grp", split_axis=1, concat_axis=1, tiled=True),
        lax.all_to_all(targets, "grp", split_axis=1, concat_axis=1, tiled=True),
    )
    own_lines = planes * depth_dev
    landing = jnp.where(arrived_at < 0, own_lines, arrived_at)
    observed = (
        jnp.zeros((view_count, own_lines + 1, width_y), jnp.float32)
        .at[view_rows, landing]
        .add(arrived)
    )
    observed = observed[:, :own_lines].reshape(view_count, planes, depth_dev, width_y)
    observed_turned = lax.all_to_all(observed, "lane", split_axis=3, concat_axis=2, tiled=True)
    current = estimate
    for sweep_at in range(ITERS):
        correction = jnp.zeros_like(current)
        for view_at in range(VIEWS):
            blurred = across_planes(current, taps_x[view_at], False)
            blurred = spread_last(blurred, taps_yz[view_at, 0], 1, False)
            turned = lax.all_to_all(blurred, "lane", split_axis=2, concat_axis=1, tiled=True)
            turned_shape = turned.shape
            flattened = spread_last(
                turned.reshape(planes, -1), taps_yz[view_at, 1], turned_shape[2], False
            )
            quotient = observed_turned[view_at].reshape(planes, -1) / flattened
            returned = spread_last(quotient, taps_yz[view_at, 1], turned_shape[2], True).reshape(
                turned_shape
            )
            returned = lax.all_to_all(returned, "lane", split_axis=1, concat_axis=2, tiled=True)
            returned = spread_last(returned, taps_yz[view_at, 0], 1, True)
            returned = across_planes(returned, taps_x[view_at], True)
            correction = correction + returned
        current = current * correction / VIEWS
    return current


def solution(mesh):
    placed = (
        P("grp", "lane", None),
        P(None, ("grp", "lane"), None),
        P(None, ("grp", "lane"), None),
        P(None, ("grp", "lane")),
        P(),
        P(),
        P(),
    )
    return jax.shard_map(
        shards, mesh=mesh, in_specs=placed, out_specs=P("grp", "lane", None), check_vma=False
    )
```

profile of v0, /device:TPU:398, one launch (start us, length us, event | category | flops | bytes accessed | tf_op | source)
XLA Modules:
  0.0 1587.2 jit_solution(8559291552776995411)
XLA Ops:
  39.6 26.9 %multiply_add_fusion.9 = f32[1,32,1024]{2,1,0:T(8,128)S(1)} fusion(f32[1,32,1024]{2,1,0:T(8,128)S(1)} %reshape.1254, f32[]{:T(128)} %bitcast.323, f32[]{:T(128)} %bitcast.322, f32[]{:T(128)} %bitcast.321, f32[]{:T(128)} %bitcast.320, f32[]{:T(128)} %bitcast.319, f32[]{:T(128)} %bitcast.318, f32[]{:T(128)} %bitcast.317, f32[]{:T(128)} %bitcast.316, ...), kind=kLoop, calls=%fused_computation.917 | loop fusion | flops 2654208 | bytes 262308 | tf_op jit(solution)/shard_map/add | solution.py:29
  70.3 17.1 %all-to-all-start.9 = ((f32[32,1,1024]{2,1,0:T(1,128)}), f32[32,1,1024]{2,1,0:T(1,128)S(1)}, u32[]{:S(2)}, u32[]{:S(2)}) async-start(f32[32,1,1024]{2,1,0:T(1,128)} %reshape.1410), calls=%async_computation.9 | async-start | bytes 262144 | tf_op jit(solution)/shard_map/all_to_all | solution.py:101
  88.2 26.6 %multiply_add_fusion.11 = f32[1,32,1024]{2,1,0:T(8,128)S(1)} fusion(f32[1,32,1024]{2,1,0:T(8,128)S(1)} %reshape.1250, f32[]{:T(128)} %bitcast.233, f32[]{:T(128)} %bitcast.232, f32[]{:T(128)} %bitcast.231, f32[]{:T(128)} %bitcast.230, f32[]{:T(128)} %bitcast.229, f32[]{:T(128)} %bitcast.228, f32[]{:T(128)} %bitcast.227, f32[]{:T(128)} %bitcast.226, ...), kind=kLoop, calls=%fused_computation.1106 | loop fusion | flops 2654208 | bytes 262308 | tf_op jit(solution)/shard_map/add | solution.py:29
  118.0 17.6 %all-to-all-start.7 = ((f32[32,1,1024]{2,1,0:T(1,128)}), f32[32,1,1024]{2,1,0:T(1,128)S(1)}, u32[]{:S(2)}, u32[]{:S(2)}) async-start(f32[32,1,1024]{2,1,0:T(1,128)} %reshape.1414), calls=%async_computation.7 | async-start | bytes 262144 | tf_op jit(solution)/shard_map/all_to_all | solution.py:101
  137.5 26.8 %multiply_add_fusion.13 = f32[1,32,1024]{2,1,0:T(8,128)S(1)} fusion(f32[1,32,1024]{2,1,0:T(8,128)S(1)} %reshape.1246, f32[]{:T(128)} %bitcast.143, f32[]{:T(128)} %bitcast.142, f32[]{:T(128)} %bitcast.141, f32[]{:T(128)} %bitcast.140, f32[]{:T(128)} %bitcast.139, f32[]{:T(128)} %bitcast.138, f32[]{:T(128)} %bitcast.137, f32[]{:T(128)} %bitcast.136, ...), kind=kLoop, calls=%fused_computation.1295 | loop fusion | flops 2654208 | bytes 262308 | tf_op jit(solution)/shard_map/add | solution.py:29
  167.5 17.0 %all-to-all-start.5 = ((f32[32,1,1024]{2,1,0:T(1,128)}), f32[32,1,1024]{2,1,0:T(1,128)S(1)}, u32[]{:S(2)}, u32[]{:S(2)}) async-start(f32[32,1,1024]{2,1,0:T(1,128)} %reshape.1418), calls=%async_computation.5 | async-start | bytes 262144 | tf_op jit(solution)/shard_map/all_to_all | solution.py:101
  214.1 27.1 %multiply_add_fusion.15 = f32[1,32,1024]{2,1,0:T(8,128)S(1)} fusion(f32[1,32,1024]{2,1,0:T(8,128)S(1)} %reshape.1242, f32[]{:T(128)} %bitcast.53, f32[]{:T(128)} %bitcast.52, f32[]{:T(128)} %bitcast.51, f32[]{:T(128)} %bitcast.50, f32[]{:T(128)} %bitcast.49, f32[]{:T(128)} %bitcast.48, f32[]{:T(128)} %bitcast.47, f32[]{:T(128)} %bitcast.46, f32[]{:T(128)} %bitcast.45, ...), kind=kLoop, calls=%fused_computation.1484 | loop fusion | flops 2654208 | bytes 262308 | tf_op jit(solution)/shard_map/add | solution.py:29
  258.8 17.1 %all-to-all-start.3 = ((f32[32,1,1024]{2,1,0:T(1,128)}), f32[32,1,1024]{2,1,0:T(1,128)}, u32[]{:S(2)}, u32[]{:S(2)}) async-start(f32[32,1,1024]{2,1,0:T(1,128)} %reshape.1422), calls=%async_computation.3 | async-start | bytes 262144 | tf_op jit(solution)/shard_map/all_to_all | solution.py:101
  294.8 17.3 %all-to-all-start.2 = ((f32[32,1,4096]{2,1,0:T(1,128)}), f32[32,1,4096]{2,1,0:T(1,128)S(1)}, u32[]{:S(2)}, u32[]{:S(2)}) async-start(f32[32,1,4096]{2,1,0:T(1,128)} %reshape.1408), calls=%async_computation.2 | async-start | bytes 1048576 | tf_op jit(solution)/shard_map/all_to_all | solution.py:94
  335.2 34.7 %add_divide_fusion.4 = f32[1,32768]{1,0:T(1,128)S(1)} fusion(f32[1,32768]{1,0:T(1,128)S(1)} %reshape_squeeze.19, f32[1,32768]{1,0:T(1,128)S(1)} %reshape.1255, f32[]{:T(128)} %bitcast.365, f32[]{:T(128)} %bitcast.364, f32[]{:T(128)} %bitcast.363, f32[]{:T(128)} %bitcast.362, f32[]{:T(128)} %bitcast.361, f32[]{:T(128)} %bitcast.360, f32[]{:T(128)} %bitcast.359, ...), kind=kLoop, calls=%fused_computation.914 | loop fusion | flops 2686976 | bytes 393380 | tf_op jit(solution)/shard_map/div | solution.py:106
  369.9 34.4 %add_reduce_fusion.8 = f32[32768]{0:T(1024)S(1)} fusion(f32[1,32768]{1,0:T(1,128)S(1)} %add_divide_fusion.4, f32[]{:T(128)} %bitcast.365, f32[]{:T(128)} %bitcast.364, f32[]{:T(128)} %bitcast.363, f32[]{:T(128)} %bitcast.362, f32[]{:T(128)} %bitcast.361, f32[]{:T(128)} %bitcast.360, f32[]{:T(128)} %bitcast.359, f32[]{:T(128)} %bitcast.358, f32[]{:T(128)} %bitcast.357, ...), kind=kLoop, calls=%fused_computation.911 | loop fusion | flops 2654208 | bytes 262308 | tf_op jit(solution)/shard_map/add | solution.py:29
  407.4 17.4 %all-to-all-start.10 = ((f32[32,1,1024]{2,1,0:T(1,128)}), f32[32,1,1024]{2,1,0:T(1,128)S(1)}, u32[]{:S(2)}, u32[]{:S(2)}) async-start(f32[32,1,1024]{2,1,0:T(1,128)} %reshape.1412), calls=%async_computation.10 | async-start | bytes 262144 | tf_op jit(solution)/shard_map/all_to_all | solution.py:110
  425.6 34.3 %add_divide_fusion.5 = f32[1,32768]{1,0:T(1,128)S(1)} fusion(f32[1,32768]{1,0:T(1,128)S(1)} %reshape_squeeze.18, f32[1,32768]{1,0:T(1,128)S(1)} %reshape.1251, f32[]{:T(128)} %bitcast.275, f32[]{:T(128)} %bitcast.274, f32[]{:T(128)} %bitcast.273, f32[]{:T(128)} %bitcast.272, f32[]{:T(128)} %bitcast.271, f32[]{:T(128)} %bitcast.270, f32[]{:T(128)} %bitcast.269, ...), kind=kLoop, calls=%fused_computation.1103 | loop fusion | flops 2686976 | bytes 393380 | tf_op jit(solution)/shard_map/div | solution.py:106
  459.9 33.9 %add_divide_fusion.6 = f32[1,32768]{1,0:T(1,128)S(1)} fusion(f32[1,32768]{1,0:T(1,128)S(1)} %reshape_squeeze.17, f32[1,32768]{1,0:T(1,128)S(1)} %reshape.1247, f32[]{:T(128)} %bitcast.185, f32[]{:T(128)} %bitcast.184, f32[]{:T(128)} %bitcast.183, f32[]{:T(128)} %bitcast.182, f32[]{:T(128)} %bitcast.181, f32[]{:T(128)} %bitcast.180, f32[]{:T(128)} %bitcast.179, ...), kind=kLoop, calls=%fused_computation.1292 | loop fusion | flops 2686976 | bytes 393380 | tf_op jit(solution)/shard_map/div | solution.py:106
  493.8 34.3 %add_divide_fusion.7 = f32[1,32768]{1,0:T(1,128)S(1)} fusion(f32[1,32768]{1,0:T(1,128)S(1)} %reshape_squeeze.16, f32[1,32768]{1,0:T(1,128)S(1)} %reshape.1243, f32[]{:T(128)} %bitcast.95, f32[]{:T(128)} %bitcast.94, f32[]{:T(128)} %bitcast.93, f32[]{:T(128)} %bitcast.92, f32[]{:T(128)} %bitcast.91, f32[]{:T(128)} %bitcast.90, f32[]{:T(128)} %bitcast.89, ...), kind=kLoop, calls=%fused_computation.1481 | loop fusion | flops 2686976 | bytes 393380 | tf_op jit(solution)/shard_map/div | solution.py:106
  528.2 34.6 %add_reduce_fusion.10 = f32[32768]{0:T(1024)S(1)} fusion(f32[1,32768]{1,0:T(1,128)S(1)} %add_divide_fusion.5, f32[]{:T(128)} %bitcast.275, f32[]{:T(128)} %bitcast.274, f32[]{:T(128)} %bitcast.273, f32[]{:T(128)} %bitcast.272, f32[]{:T(128)} %bitcast.271, f32[]{:T(128)} %bitcast.270, f32[]{:T(128)} %bitcast.269, f32[]{:T(128)} %bitcast.268, f32[]{:T(128)} %bitcast.267, ...), kind=kLoop, calls=%fused_computation.1100 | loop fusion | flops 2654208 | bytes 262308 | tf_op jit(solution)/shard_map/add | solution.py:29
  565.8 17.0 %all-to-all-start.8 = ((f32[32,1,1024]{2,1,0:T(1,128)}), f32[32,1,1024]{2,1,0:T(1,128)S(1)}, u32[]{:S(2)}, u32[]{:S(2)}) async-start(f32[32,1,1024]{2,1,0:T(1,128)} %reshape.1416), calls=%async_computation.8 | async-start | bytes 262144 | tf_op jit(solution)/shard_map/all_to_all | solution.py:110
  582.9 33.8 %add_reduce_fusion.12 = f32[32768]{0:T(1024)S(1)} fusion(f32[1,32768]{1,0:T(1,128)S(1)} %add_divide_fusion.6, f32[]{:T(128)} %bitcast.185, f32[]{:T(128)} %bitcast.184, f32[]{:T(128)} %bitcast.183, f32[]{:T(128)} %bitcast.182, f32[]{:T(128)} %bitcast.181, f32[]{:T(128)} %bitcast.180, f32[]{:T(128)} %bitcast.179, f32[]{:T(128)} %bitcast.178, f32[]{:T(128)} %bitcast.177, ...), kind=kLoop, calls=%fused_computation.1289 | loop fusion | flops 2654208 | bytes 262308 | tf_op jit(solution)/shard_map/add | solution.py:29
  619.8 17.3 %all-to-all-start.6 = ((f32[32,1,1024]{2,1,0:T(1,128)}), f32[32,1,1024]{2,1,0:T(1,128)S(1)}, u32[]{:S(2)}, u32[]{:S(2)}) async-start(f32[32,1,1024]{2,1,0:T(1,128)} %reshape.1420), calls=%async_computation.6 | async-start | bytes 262144 | tf_op jit(solution)/shard_map/all_to_all | solution.py:110
  637.1 34.2 %add_reduce_fusion.14 = f32[32768]{0:T(1024)S(1)} fusion(f32[1,32768]{1,0:T(1,128)S(1)} %add_divide_fusion.7, f32[]{:T(128)} %bitcast.95, f32[]{:T(128)} %bitcast.94, f32[]{:T(128)} %bitcast.93, f32[]{:T(128)} %bitcast.92, f32[]{:T(128)} %bitcast.91, f32[]{:T(128)} %bitcast.90, f32[]{:T(128)} %bitcast.89, f32[]{:T(128)} %bitcast.88, f32[]{:T(128)} %bitcast.87, ...), kind=kLoop, calls=%fused_computation.1478 | loop fusion | flops 2654208 | bytes 262308 | tf_op jit(solution)/shard_map/add | solution.py:29
  677.6 17.0 %all-to-all-start.4 = ((f32[32,1,1024]{2,1,0:T(1,128)}), f32[32,1,1024]{2,1,0:T(1,128)S(1)}, u32[]{:S(2)}, u32[]{:S(2)}) async-start(f32[32,1,1024]{2,1,0:T(1,128)} %reshape.1424), calls=%async_computation.4 | async-start | bytes 262144 | tf_op jit(solution)/shard_map/all_to_all | solution.py:110
  694.6 26.9 %multiply_add_fusion.8 = f32[1,32,1024]{2,1,0:T(8,128)S(1)} fusion(f32[1,32,1024]{2,1,0:T(8,128)S(1)} %all_to_all.248, f32[]{:T(128)} %bitcast.323, f32[]{:T(128)} %bitcast.322, f32[]{:T(128)} %bitcast.321, f32[]{:T(128)} %bitcast.320, f32[]{:T(128)} %bitcast.319, f32[]{:T(128)} %bitcast.318, f32[]{:T(128)} %bitcast.317, f32[]{:T(128)} %bitcast.316, ...), kind=kLoop, calls=%fused_computation.820 | loop fusion | flops 2654208 | bytes 262308 | tf_op jit(solution)/shard_map/add | solution.py:29
  729.1 26.6 %multiply_add_fusion.10 = f32[1,32,1024]{2,1,0:T(8,128)S(1)} fusion(f32[1,32,1024]{2,1,0:T(8,128)S(1)} %all_to_all.241, f32[]{:T(128)} %bitcast.233, f32[]{:T(128)} %bitcast.232, f32[]{:T(128)} %bitcast.231, f32[]{:T(128)} %bitcast.230, f32[]{:T(128)} %bitcast.229, f32[]{:T(128)} %bitcast.228, f32[]{:T(128)} %bitcast.227, f32[]{:T(128)} %bitcast.226, ...), kind=kLoop, calls=%fused_computation.1009 | loop fusion | flops 2654208 | bytes 262308 | tf_op jit(solution)/shard_map/add | solution.py:29
  766.6 26.8 %multiply_add_fusion.12 = f32[1,32,1024]{2,1,0:T(8,128)S(1)} fusion(f32[1,32,1024]{2,1,0:T(8,128)S(1)} %all_to_all.234, f32[]{:T(128)} %bitcast.143, f32[]{:T(128)} %bitcast.142, f32[]{:T(128)} %bitcast.141, f32[]{:T(128)} %bitcast.140, f32[]{:T(128)} %bitcast.139, f32[]{:T(128)} %bitcast.138, f32[]{:T(128)} %bitcast.137, f32[]{:T(128)} %bitcast.136, ...), kind=kLoop, calls=%fused_computation.1198 | loop fusion | flops 2654208 | bytes 262308 | tf_op jit(solution)/shard_map/add | solution.py:29
  800.5 27.1 %multiply_add_fusion.14 = f32[1,32,1024]{2,1,0:T(8,128)S(1)} fusion(f32[1,32,1024]{2,1,0:T(8,128)S(1)} %all_to_all.227, f32[]{:T(128)} %bitcast.53, f32[]{:T(128)} %bitcast.52, f32[]{:T(128)} %bitcast.51, f32[]{:T(128)} %bitcast.50, f32[]{:T(128)} %bitcast.49, f32[]{:T(128)} %bitcast.48, f32[]{:T(128)} %bitcast.47, f32[]{:T(128)} %bitcast.46, f32[]{:T(128)} %bitcast.45, ...), kind=kLoop, calls=%fused_computation.1387 | loop fusion | flops 2654208 | bytes 262308 | tf_op jit(solution)/shard_map/add | solution.py:29
  870.4 26.9 %multiply_add_fusion.1 = f32[1,32,1024]{2,1,0:T(8,128)S(1)} fusion(f32[1,32,1024]{2,1,0:T(8,128)S(1)} %reshape.1271, f32[]{:T(128)} %bitcast.323, f32[]{:T(128)} %bitcast.322, f32[]{:T(128)} %bitcast.321, f32[]{:T(128)} %bitcast.320, f32[]{:T(128)} %bitcast.319, f32[]{:T(128)} %bitcast.318, f32[]{:T(128)} %bitcast.317, f32[]{:T(128)} %bitcast.316, ...), kind=kLoop, calls=%fused_computation.160 | loop fusion | flops 2654208 | bytes 262308 | tf_op jit(solution)/shard_map/add | solution.py:29
  917.6 26.6 %multiply_add_fusion.3 = f32[1,32,1024]{2,1,0:T(8,128)S(1)} fusion(f32[1,32,1024]{2,1,0:T(8,128)S(1)} %reshape.1267, f32[]{:T(128)} %bitcast.233, f32[]{:T(128)} %bitcast.232, f32[]{:T(128)} %bitcast.231, f32[]{:T(128)} %bitcast.230, f32[]{:T(128)} %bitcast.229, f32[]{:T(128)} %bitcast.228, f32[]{:T(128)} %bitcast.227, f32[]{:T(128)} %bitcast.226, ...), kind=kLoop, calls=%fused_computation.349 | loop fusion | flops 2654208 | bytes 262308 | tf_op jit(solution)/shard_map/add | solution.py:29
  947.5 26.8 %multiply_add_fusion.5 = f32[1,32,1024]{2,1,0:T(8,128)S(1)} fusion(f32[1,32,1024]{2,1,0:T(8,128)S(1)} %reshape.1263, f32[]{:T(128)} %bitcast.143, f32[]{:T(128)} %bitcast.142, f32[]{:T(128)} %bitcast.141, f32[]{:T(128)} %bitcast.140, f32[]{:T(128)} %bitcast.139, f32[]{:T(128)} %bitcast.138, f32[]{:T(128)} %bitcast.137, f32[]{:T(128)} %bitcast.136, ...), kind=kLoop, calls=%fused_computation.538 | loop fusion | flops 2654208 | bytes 262308 | tf_op jit(solution)/shard_map/add | solution.py:29
  977.6 27.1 %multiply_add_fusion.7 = f32[1,32,1024]{2,1,0:T(8,128)S(1)} fusion(f32[1,32,1024]{2,1,0:T(8,128)S(1)} %reshape.1259, f32[]{:T(128)} %bitcast.53, f32[]{:T(128)} %bitcast.52, f32[]{:T(128)} %bitcast.51, f32[]{:T(128)} %bitcast.50, f32[]{:T(128)} %bitcast.49, f32[]{:T(128)} %bitcast.48, f32[]{:T(128)} %bitcast.47, f32[]{:T(128)} %bitcast.46, f32[]{:T(128)} %bitcast.45, ...), kind=kLoop, calls=%fused_computation.727 | loop fusion | flops 2654208 | bytes 262308 | tf_op jit(solution)/shard_map/add | solution.py:29
  1007.9 17.4 %all-to-all-start.15 = ((f32[32,1,1024]{2,1,0:T(1,128)}), f32[32,1,1024]{2,1,0:T(1,128)S(1)}, u32[]{:S(2)}, u32[]{:S(2)}) async-start(f32[32,1,1024]{2,1,0:T(1,128)} %reshape.1430), calls=%async_computation.15 | async-start | bytes 262144 | tf_op jit(solution)/shard_map/all_to_all | solution.py:101
  1028.2 34.5 %add_divide_fusion = f32[1,32768]{1,0:T(1,128)S(1)} fusion(f32[1,32768]{1,0:T(1,128)S(1)} %reshape_squeeze.19, f32[1,32768]{1,0:T(1,128)S(1)} %reshape.1272, f32[]{:T(128)} %bitcast.365, f32[]{:T(128)} %bitcast.364, f32[]{:T(128)} %bitcast.363, f32[]{:T(128)} %bitcast.362, f32[]{:T(128)} %bitcast.361, f32[]{:T(128)} %bitcast.360, f32[]{:T(128)} %bitcast.359, ...), kind=kLoop, calls=%fused_computation.157 | loop fusion | flops 2686976 | bytes 393380 | tf_op jit(solution)/shard_map/div | solution.py:106
  1062.7 17.0 %all-to-all-start.13 = ((f32[32,1,1024]{2,1,0:T(1,128)}), f32[32,1,1024]{2,1,0:T(1,128)S(1)}, u32[]{:S(2)}, u32[]{:S(2)}) async-start(f32[32,1,1024]{2,1,0:T(1,128)} %reshape.1434), calls=%async_computation.13 | async-start | bytes 262144 | tf_op jit(solution)/shard_map/all_to_all | solution.py:101
  1082.7 34.3 %add_divide_fusion.1 = f32[1,32768]{1,0:T(1,128)S(1)} fusion(f32[1,32768]{1,0:T(1,128)S(1)} %reshape_squeeze.18, f32[1,32768]{1,0:T(1,128)S(1)} %reshape.1268, f32[]{:T(128)} %bitcast.275, f32[]{:T(128)} %bitcast.274, f32[]{:T(128)} %bitcast.273, f32[]{:T(128)} %bitcast.272, f32[]{:T(128)} %bitcast.271, f32[]{:T(128)} %bitcast.270, f32[]{:T(128)} %bitcast.269, ...), kind=kLoop, calls=%fused_computation.346 | loop fusion | flops 2686976 | bytes 393380 | tf_op jit(solution)/shard_map/div | solution.py:106
  1117.0 17.6 %all-to-all-start.11 = ((f32[32,1,1024]{2,1,0:T(1,128)}), f32[32,1,1024]{2,1,0:T(1,128)S(1)}, u32[]{:S(2)}, u32[]{:S(2)}) async-start(f32[32,1,1024]{2,1,0:T(1,128)} %reshape.1438), calls=%async_computation.11 | async-start | bytes 262144 | tf_op jit(solution)/shard_map/all_to_all | solution.py:101
  1137.5 33.9 %add_divide_fusion.2 = f32[1,32768]{1,0:T(1,128)S(1)} fusion(f32[1,32768]{1,0:T(1,128)S(1)} %reshape_squeeze.17, f32[1,32768]{1,0:T(1,128)S(1)} %reshape.1264, f32[]{:T(128)} %bitcast.185, f32[]{:T(128)} %bitcast.184, f32[]{:T(128)} %bitcast.183, f32[]{:T(128)} %bitcast.182, f32[]{:T(128)} %bitcast.181, f32[]{:T(128)} %bitcast.180, f32[]{:T(128)} %bitcast.179, ...), kind=kLoop, calls=%fused_computation.535 | loop fusion | flops 2686976 | bytes 393380 | tf_op jit(solution)/shard_map/div | solution.py:106
  1171.4 34.4 %add_reduce_fusion = f32[32768]{0:T(1024)S(1)} fusion(f32[1,32768]{1,0:T(1,128)S(1)} %add_divide_fusion, f32[]{:T(128)} %bitcast.365, f32[]{:T(128)} %bitcast.364, f32[]{:T(128)} %bitcast.363, f32[]{:T(128)} %bitcast.362, f32[]{:T(128)} %bitcast.361, f32[]{:T(128)} %bitcast.360, f32[]{:T(128)} %bitcast.359, f32[]{:T(128)} %bitcast.358, f32[]{:T(128)} %bitcast.357, ...), kind=kLoop, calls=%fused_computation.154 | loop fusion | flops 2654208 | bytes 262308 | tf_op jit(solution)/shard_map/add | solution.py:29
  1208.9 17.3 %all-to-all-start.18 = ((f32[32,1,1024]{2,1,0:T(1,128)}), f32[32,1,1024]{2,1,0:T(1,128)S(1)}, u32[]{:S(2)}, u32[]{:S(2)}) async-start(f32[32,1,1024]{2,1,0:T(1,128)} %reshape.1428), calls=%async_computation.18 | async-start | bytes 262144 | tf_op jit(solution)/shard_map/all_to_all | solution.py:110
  1229.1 34.3 %add_divide_fusion.3 = f32[1,32768]{1,0:T(1,128)S(1)} fusion(f32[1,32768]{1,0:T(1,128)S(1)} %reshape_squeeze.16, f32[1,32768]{1,0:T(1,128)S(1)} %reshape.1260, f32[]{:T(128)} %bitcast.95, f32[]{:T(128)} %bitcast.94, f32[]{:T(128)} %bitcast.93, f32[]{:T(128)} %bitcast.92, f32[]{:T(128)} %bitcast.91, f32[]{:T(128)} %bitcast.90, f32[]{:T(128)} %bitcast.89, ...), kind=kLoop, calls=%fused_computation.724 | loop fusion | flops 2686976 | bytes 393380 | tf_op jit(solution)/shard_map/div | solution.py:106
  1263.5 34.1 %add_reduce_fusion.2 = f32[32768]{0:T(1024)S(1)} fusion(f32[1,32768]{1,0:T(1,128)S(1)} %add_divide_fusion.1, f32[]{:T(128)} %bitcast.275, f32[]{:T(128)} %bitcast.274, f32[]{:T(128)} %bitcast.273, f32[]{:T(128)} %bitcast.272, f32[]{:T(128)} %bitcast.271, f32[]{:T(128)} %bitcast.270, f32[]{:T(128)} %bitcast.269, f32[]{:T(128)} %bitcast.268, f32[]{:T(128)} %bitcast.267, ...), kind=kLoop, calls=%fused_computation.343 | loop fusion | flops 2654208 | bytes 262308 | tf_op jit(solution)/shard_map/add | solution.py:29
  1300.7 17.4 %all-to-all-start.16 = ((f32[32,1,1024]{2,1,0:T(1,128)}), f32[32,1,1024]{2,1,0:T(1,128)S(1)}, u32[]{:S(2)}, u32[]{:S(2)}) async-start(f32[32,1,1024]{2,1,0:T(1,128)} %reshape.1432), calls=%async_computation.16 | async-start | bytes 262144 | tf_op jit(solution)/shard_map/all_to_all | solution.py:110
  1318.1 33.8 %add_reduce_fusion.4 = f32[32768]{0:T(1024)S(1)} fusion(f32[1,32768]{1,0:T(1,128)S(1)} %add_divide_fusion.2, f32[]{:T(128)} %bitcast.185, f32[]{:T(128)} %bitcast.184, f32[]{:T(128)} %bitcast.183, f32[]{:T(128)} %bitcast.182, f32[]{:T(128)} %bitcast.181, f32[]{:T(128)} %bitcast.180, f32[]{:T(128)} %bitcast.179, f32[]{:T(128)} %bitcast.178, f32[]{:T(128)} %bitcast.177, ...), kind=kLoop, calls=%fused_computation.532 | loop fusion | flops 2654208 | bytes 262308 | tf_op jit(solution)/shard_map/add | solution.py:29
  1355.0 17.0 %all-to-all-start.14 = ((f32[32,1,1024]{2,1,0:T(1,128)}), f32[32,1,1024]{2,1,0:T(1,128)S(1)}, u32[]{:S(2)}, u32[]{:S(2)}) async-start(f32[32,1,1024]{2,1,0:T(1,128)} %reshape.1436), calls=%async_computation.14 | async-start | bytes 262144 | tf_op jit(solution)/shard_map/all_to_all | solution.py:110
  1372.0 34.2 %add_reduce_fusion.6 = f32[32768]{0:T(1024)S(1)} fusion(f32[1,32768]{1,0:T(1,128)S(1)} %add_divide_fusion.3, f32[]{:T(128)} %bitcast.95, f32[]{:T(128)} %bitcast.94, f32[]{:T(128)} %bitcast.93, f32[]{:T(128)} %bitcast.92, f32[]{:T(128)} %bitcast.91, f32[]{:T(128)} %bitcast.90, f32[]{:T(128)} %bitcast.89, f32[]{:T(128)} %bitcast.88, f32[]{:T(128)} %bitcast.87, ...), kind=kLoop, calls=%fused_computation.721 | loop fusion | flops 2654208 | bytes 262308 | tf_op jit(solution)/shard_map/add | solution.py:29
  1412.5 17.6 %all-to-all-start.12 = ((f32[32,1,1024]{2,1,0:T(1,128)}), f32[32,1,1024]{2,1,0:T(1,128)S(1)}, u32[]{:S(2)}, u32[]{:S(2)}) async-start(f32[32,1,1024]{2,1,0:T(1,128)} %reshape.1440), calls=%async_computation.12 | async-start | bytes 262144 | tf_op jit(solution)/shard_map/all_to_all | solution.py:110
  1430.1 26.9 %multiply_add_fusion = f32[1,32,1024]{2,1,0:T(8,128)S(1)} fusion(f32[1,32,1024]{2,1,0:T(8,128)S(1)} %all_to_all.276, f32[]{:T(128)} %bitcast.323, f32[]{:T(128)} %bitcast.322, f32[]{:T(128)} %bitcast.321, f32[]{:T(128)} %bitcast.320, f32[]{:T(128)} %bitcast.319, f32[]{:T(128)} %bitcast.318, f32[]{:T(128)} %bitcast.317, f32[]{:T(128)} %bitcast.316, ...), kind=kLoop, calls=%fused_computation.63 | loop fusion | flops 2654208 | bytes 262308 | tf_op jit(solution)/shard_map/add | solution.py:29
  1464.5 26.6 %multiply_add_fusion.2 = f32[1,32,1024]{2,1,0:T(8,128)S(1)} fusion(f32[1,32,1024]{2,1,0:T(8,128)S(1)} %all_to_all.269, f32[]{:T(128)} %bitcast.233, f32[]{:T(128)} %bitcast.232, f32[]{:T(128)} %bitcast.231, f32[]{:T(128)} %bitcast.230, f32[]{:T(128)} %bitcast.229, f32[]{:T(128)} %bitcast.228, f32[]{:T(128)} %bitcast.227, f32[]{:T(128)} %bitcast.226, ...), kind=kLoop, calls=%fused_computation.252 | loop fusion | flops 2654208 | bytes 262308 | tf_op jit(solution)/shard_map/add | solution.py:29
  1500.6 26.8 %multiply_add_fusion.4 = f32[1,32,1024]{2,1,0:T(8,128)S(1)} fusion(f32[1,32,1024]{2,1,0:T(8,128)S(1)} %all_to_all.262, f32[]{:T(128)} %bitcast.143, f32[]{:T(128)} %bitcast.142, f32[]{:T(128)} %bitcast.141, f32[]{:T(128)} %bitcast.140, f32[]{:T(128)} %bitcast.139, f32[]{:T(128)} %bitcast.138, f32[]{:T(128)} %bitcast.137, f32[]{:T(128)} %bitcast.136, ...), kind=kLoop, calls=%fused_computation.441 | loop fusion | flops 2654208 | bytes 262308 | tf_op jit(solution)/shard_map/add | solution.py:29
  1535.7 27.1 %multiply_add_fusion.6 = f32[1,32,1024]{2,1,0:T(8,128)S(1)} fusion(f32[1,32,1024]{2,1,0:T(8,128)S(1)} %all_to_all.255, f32[]{:T(128)} %bitcast.53, f32[]{:T(128)} %bitcast.52, f32[]{:T(128)} %bitcast.51, f32[]{:T(128)} %bitcast.50, f32[]{:T(128)} %bitcast.49, f32[]{:T(128)} %bitcast.48, f32[]{:T(128)} %bitcast.47, f32[]{:T(128)} %bitcast.46, f32[]{:T(128)} %bitcast.45, ...), kind=kLoop, calls=%fused_computation.630 | loop fusion | flops 2654208 | bytes 262308 | tf_op jit(solution)/shard_map/add | solution.py:29
  (318 shorter events, 338.3 us)
Async XLA Ops:
  0.0 29.7 %collective-permute-start.1 = (f32[1,32,1024]{2,1,0:T(8,128)}, f32[1,32,1024]{2,1,0:T(8,128)S(1)}, u32[]{:S(2)}, u32[]{:S(2)}) collective-permute-start(f32[1,32,1024]{2,1,0:T(8,128)} %param.7), channel_id=1, source_target_pairs={{32,0},{64,32},{96,64},{128,96},{160,128},{192,160},{224,192},{256... | collective-permute-start | bytes 393224 | tf_op jit(solution)/shard_map/ppermute | solution.py:19
  3.6 26.1 %collective-permute-start = (f32[1,32,1024]{2,1,0:T(8,128)}, f32[1,32,1024]{2,1,0:T(8,128)S(1)}, u32[]{:S(2)}, u32[]{:S(2)}) collective-permute-start(f32[1,32,1024]{2,1,0:T(8,128)} %param.7), channel_id=1, source_target_pairs={{0,32},{32,64},{64,96},{96,128},{128,160},{160,192},{192,224},{224... | collective-permute-start | bytes 393224 | tf_op jit(solution)/shard_map/ppermute | solution.py:18
  8.8 14.8 copy-start.6
  8.8 19.3 %copy-start.7 = (f32[4,3]{1,0:T(4,128)S(1)}, f32[4,3]{1,0:T(4,128)}, u32[]{:S(2)}) copy-start(f32[4,3]{1,0:T(4,128)} %param.12) | copy-start | bytes 148
  8.8 20.9 %copy-start.1 = (f32[1,32,1024]{2,1,0:T(8,128)S(1)}, f32[1,32,1024]{2,1,0:T(8,128)}, u32[]{:S(2)}) copy-start(f32[1,32,1024]{2,1,0:T(8,128)} %param.7) | copy-start | bytes 393220
  15.9 54.3 %all-to-all-start = ((s32[4,16,4]{2,0,1:T(4,128)}), s32[4,16,4]{2,0,1:T(4,128)S(1)}, u32[]{:S(2)}, u32[]{:S(2)}) async-start(s32[4,16,4]{2,0,1:T(4,128)} %copy.159), calls=%async_computation | async-start | bytes 65536 | tf_op jit(solution)/shard_map/all_to_all | solution.py:84
  30.2 57.9 %copy-start.8 = (s32[4]{0:T(128)S(1)}, s32[4]{0:T(128)}, u32[]{:S(2)}) copy-start(s32[4]{0:T(128)} %param.11) | copy-start | bytes 52
  69.3 66.3 %copy-start = (f32[4,32,1024]{2,1,0:T(8,128)S(1)}, f32[4,32,1024]{2,1,0:T(8,128)}, u32[]{:S(2)}) copy-start(f32[4,32,1024]{2,1,0:T(8,128)} %param.8) | copy-start | bytes 1572868
  70.3 47.7 %all-to-all-start.9 = ((f32[32,1,1024]{2,1,0:T(1,128)}), f32[32,1,1024]{2,1,0:T(1,128)S(1)}, u32[]{:S(2)}, u32[]{:S(2)}) async-start(f32[32,1,1024]{2,1,0:T(1,128)} %reshape.1410), calls=%async_computation.9 | async-start | bytes 262144 | tf_op jit(solution)/shard_map/all_to_all | solution.py:101
  118.0 49.5 %all-to-all-start.7 = ((f32[32,1,1024]{2,1,0:T(1,128)}), f32[32,1,1024]{2,1,0:T(1,128)S(1)}, u32[]{:S(2)}, u32[]{:S(2)}) async-start(f32[32,1,1024]{2,1,0:T(1,128)} %reshape.1414), calls=%async_computation.7 | async-start | bytes 262144 | tf_op jit(solution)/shard_map/all_to_all | solution.py:101
  167.5 32.8 %copy-start.2 = (f32[32,1,1024]{2,1,0:T(1,128)}, f32[32,1,1024]{2,1,0:T(1,128)S(1)}, u32[]{:S(2)}) copy-start(f32[32,1,1024]{2,1,0:T(1,128)S(1)} %all-to-all-done.7) | copy-start | bytes 393220
  167.5 34.5 %all-to-all-start.5 = ((f32[32,1,1024]{2,1,0:T(1,128)}), f32[32,1,1024]{2,1,0:T(1,128)S(1)}, u32[]{:S(2)}, u32[]{:S(2)}) async-start(f32[32,1,1024]{2,1,0:T(1,128)} %reshape.1418), calls=%async_computation.5 | async-start | bytes 262144 | tf_op jit(solution)/shard_map/all_to_all | solution.py:101
  202.0 41.5 %copy-start.4 = (f32[32,1,1024]{2,1,0:T(1,128)}, f32[32,1,1024]{2,1,0:T(1,128)S(1)}, u32[]{:S(2)}) copy-start(f32[32,1,1024]{2,1,0:T(1,128)S(1)} %all-to-all-done.5) | copy-start | bytes 393220
  202.0 56.8 %all-to-all-start.1 = ((f32[4,64,1024]{2,0,1:T(4,128)}), f32[4,64,1024]{2,0,1:T(4,128)S(1)}, u32[]{:S(2)}, u32[]{:S(2)}) async-start(f32[4,64,1024]{2,0,1:T(4,128)} %copy.162), calls=%async_computation.1 | async-start | bytes 2097152 | tf_op jit(solution)/shard_map/all_to_all | solution.py:83
  258.8 36.0 %all-to-all-start.3 = ((f32[32,1,1024]{2,1,0:T(1,128)}), f32[32,1,1024]{2,1,0:T(1,128)}, u32[]{:S(2)}, u32[]{:S(2)}) async-start(f32[32,1,1024]{2,1,0:T(1,128)} %reshape.1422), calls=%async_computation.3 | async-start | bytes 262144 | tf_op jit(solution)/shard_map/all_to_all | solution.py:101
  294.8 33.6 %all-to-all-start.2 = ((f32[32,1,4096]{2,1,0:T(1,128)}), f32[32,1,4096]{2,1,0:T(1,128)S(1)}, u32[]{:S(2)}, u32[]{:S(2)}) async-start(f32[32,1,4096]{2,1,0:T(1,128)} %reshape.1408), calls=%async_computation.2 | async-start | bytes 1048576 | tf_op jit(solution)/shard_map/all_to_all | solution.py:94
  312.1 6.6 copy-start.3
  318.4 3.2 copy-start.5
  407.4 158.4 %all-to-all-start.10 = ((f32[32,1,1024]{2,1,0:T(1,128)}), f32[32,1,1024]{2,1,0:T(1,128)S(1)}, u32[]{:S(2)}, u32[]{:S(2)}) async-start(f32[32,1,1024]{2,1,0:T(1,128)} %reshape.1412), calls=%async_computation.10 | async-start | bytes 262144 | tf_op jit(solution)/shard_map/all_to_all | solution.py:110
  565.8 53.9 %all-to-all-start.8 = ((f32[32,1,1024]{2,1,0:T(1,128)}), f32[32,1,1024]{2,1,0:T(1,128)S(1)}, u32[]{:S(2)}, u32[]{:S(2)}) async-start(f32[32,1,1024]{2,1,0:T(1,128)} %reshape.1416), calls=%async_computation.8 | async-start | bytes 262144 | tf_op jit(solution)/shard_map/all_to_all | solution.py:110
  619.8 57.8 %all-to-all-start.6 = ((f32[32,1,1024]{2,1,0:T(1,128)}), f32[32,1,1024]{2,1,0:T(1,128)S(1)}, u32[]{:S(2)}, u32[]{:S(2)}) async-start(f32[32,1,1024]{2,1,0:T(1,128)} %reshape.1420), calls=%async_computation.6 | async-start | bytes 262144 | tf_op jit(solution)/shard_map/all_to_all | solution.py:110
  677.6 119.7 %all-to-all-start.4 = ((f32[32,1,1024]{2,1,0:T(1,128)}), f32[32,1,1024]{2,1,0:T(1,128)S(1)}, u32[]{:S(2)}, u32[]{:S(2)}) async-start(f32[32,1,1024]{2,1,0:T(1,128)} %reshape.1424), calls=%async_computation.4 | async-start | bytes 262144 | tf_op jit(solution)/shard_map/all_to_all | solution.py:110
  721.6 106.1 %collective-permute-start.9 = (f32[1,32,1024]{2,1,0:T(8,128)S(1)}, f32[1,32,1024]{2,1,0:T(8,128)S(1)}, u32[]{:S(2)}, u32[]{:S(2)}) collective-permute-start(f32[1,32,1024]{2,1,0:T(8,128)S(1)} %multiply_add_fusion.8), channel_id=1, source_target_pairs={{32,0},{64,32},{96,64},{128,96},{160,128},{192,160},{224,192},{256... | collective-permute-start | bytes 393224 | tf_op jit(solution)/shard_map/ppermute | solution.py:19
  723.5 106.1 %collective-permute-start.8 = (f32[1,32,1024]{2,1,0:T(8,128)S(1)}, f32[1,32,1024]{2,1,0:T(8,128)S(1)}, u32[]{:S(2)}, u32[]{:S(2)}) collective-permute-start(f32[1,32,1024]{2,1,0:T(8,128)S(1)} %multiply_add_fusion.8), channel_id=1, source_target_pairs={{0,32},{32,64},{64,96},{96,128},{128,160},{160,192},{192,224},{224... | collective-permute-start | bytes 393224 | tf_op jit(solution)/shard_map/ppermute | solution.py:18
  755.7 78.8 %collective-permute-start.7 = (f32[1,32,1024]{2,1,0:T(8,128)S(1)}, f32[1,32,1024]{2,1,0:T(8,128)S(1)}, u32[]{:S(2)}, u32[]{:S(2)}) collective-permute-start(f32[1,32,1024]{2,1,0:T(8,128)S(1)} %multiply_add_fusion.10), channel_id=1, source_target_pairs={{32,0},{64,32},{96,64},{128,96},{160,128},{192,160},{224,192},{256... | collective-permute-start | bytes 393224 | tf_op jit(solution)/shard_map/ppermute | solution.py:19
  760.1 76.3 %collective-permute-start.6 = (f32[1,32,1024]{2,1,0:T(8,128)S(1)}, f32[1,32,1024]{2,1,0:T(8,128)S(1)}, u32[]{:S(2)}, u32[]{:S(2)}) collective-permute-start(f32[1,32,1024]{2,1,0:T(8,128)S(1)} %multiply_add_fusion.10), channel_id=1, source_target_pairs={{0,32},{32,64},{64,96},{96,128},{128,160},{160,192},{192,224},{224... | collective-permute-start | bytes 393224 | tf_op jit(solution)/shard_map/ppermute | solution.py:18
  793.5 43.9 %collective-permute-start.5 = (f32[1,32,1024]{2,1,0:T(8,128)S(1)}, f32[1,32,1024]{2,1,0:T(8,128)S(1)}, u32[]{:S(2)}, u32[]{:S(2)}) collective-permute-start(f32[1,32,1024]{2,1,0:T(8,128)S(1)} %multiply_add_fusion.12), channel_id=1, source_target_pairs={{32,0},{64,32},{96,64},{128,96},{160,128},{192,160},{224,192},{256... | collective-permute-start | bytes 393224 | tf_op jit(solution)/shard_map/ppermute | solution.py:19
  827.6 9.8 collective-permute-start.4
  829.6 8.4 collective-permute-start.3
  834.5 7.5 collective-permute-start.2
  851.1 4.5 collective-permute-start.11
  853.1 7.5 collective-permute-start.10
  900.5 107.3 %all-to-all-start.17 = ((f32[32,1,1024]{2,1,0:T(1,128)}), f32[32,1,1024]{2,1,0:T(1,128)S(1)}, u32[]{:S(2)}, u32[]{:S(2)}) async-start(f32[32,1,1024]{2,1,0:T(1,128)} %reshape.1426), calls=%async_computation.17 | async-start | bytes 262144 | tf_op jit(solution)/shard_map/all_to_all | solution.py:101
  1007.9 54.8 %all-to-all-start.15 = ((f32[32,1,1024]{2,1,0:T(1,128)}), f32[32,1,1024]{2,1,0:T(1,128)S(1)}, u32[]{:S(2)}, u32[]{:S(2)}) async-start(f32[32,1,1024]{2,1,0:T(1,128)} %reshape.1430), calls=%async_computation.15 | async-start | bytes 262144 | tf_op jit(solution)/shard_map/all_to_all | solution.py:101
  1062.7 54.3 %all-to-all-start.13 = ((f32[32,1,1024]{2,1,0:T(1,128)}), f32[32,1,1024]{2,1,0:T(1,128)S(1)}, u32[]{:S(2)}, u32[]{:S(2)}) async-start(f32[32,1,1024]{2,1,0:T(1,128)} %reshape.1434), calls=%async_computation.13 | async-start | bytes 262144 | tf_op jit(solution)/shard_map/all_to_all | solution.py:101
  1117.0 91.9 %all-to-all-start.11 = ((f32[32,1,1024]{2,1,0:T(1,128)}), f32[32,1,1024]{2,1,0:T(1,128)S(1)}, u32[]{:S(2)}, u32[]{:S(2)}) async-start(f32[32,1,1024]{2,1,0:T(1,128)} %reshape.1438), calls=%async_computation.11 | async-start | bytes 262144 | tf_op jit(solution)/shard_map/all_to_all | solution.py:101
  1208.9 91.8 %all-to-all-start.18 = ((f32[32,1,1024]{2,1,0:T(1,128)}), f32[32,1,1024]{2,1,0:T(1,128)S(1)}, u32[]{:S(2)}, u32[]{:S(2)}) async-start(f32[32,1,1024]{2,1,0:T(1,128)} %reshape.1428), calls=%async_computation.18 | async-start | bytes 262144 | tf_op jit(solution)/shard_map/all_to_all | solution.py:110
  1300.7 54.3 %all-to-all-start.16 = ((f32[32,1,1024]{2,1,0:T(1,128)}), f32[32,1,1024]{2,1,0:T(1,128)S(1)}, u32[]{:S(2)}, u32[]{:S(2)}) async-start(f32[32,1,1024]{2,1,0:T(1,128)} %reshape.1432), calls=%async_computation.16 | async-start | bytes 262144 | tf_op jit(solution)/shard_map/all_to_all | solution.py:110
  1355.0 57.5 %all-to-all-start.14 = ((f32[32,1,1024]{2,1,0:T(1,128)}), f32[32,1,1024]{2,1,0:T(1,128)S(1)}, u32[]{:S(2)}, u32[]{:S(2)}) async-start(f32[32,1,1024]{2,1,0:T(1,128)} %reshape.1436), calls=%async_computation.14 | async-start | bytes 262144 | tf_op jit(solution)/shard_map/all_to_all | solution.py:110
  1412.5 120.0 %all-to-all-start.12 = ((f32[32,1,1024]{2,1,0:T(1,128)}), f32[32,1,1024]{2,1,0:T(1,128)S(1)}, u32[]{:S(2)}, u32[]{:S(2)}) async-start(f32[32,1,1024]{2,1,0:T(1,128)} %reshape.1440), calls=%async_computation.12 | async-start | bytes 262144 | tf_op jit(solution)/shard_map/all_to_all | solution.py:110
  1457.0 105.8 %collective-permute-start.19 = (f32[1,32,1024]{2,1,0:T(8,128)S(1)}, f32[1,32,1024]{2,1,0:T(8,128)S(1)}, u32[]{:S(2)}, u32[]{:S(2)}) collective-permute-start(f32[1,32,1024]{2,1,0:T(8,128)S(1)} %multiply_add_fusion), channel_id=1, source_target_pairs={{32,0},{64,32},{96,64},{128,96},{160,128},{192,160},{224,192},{256... | collective-permute-start | bytes 393224 | tf_op jit(solution)/shard_map/ppermute | solution.py:19
  1458.9 105.8 %collective-permute-start.18 = (f32[1,32,1024]{2,1,0:T(8,128)S(1)}, f32[1,32,1024]{2,1,0:T(8,128)S(1)}, u32[]{:S(2)}, u32[]{:S(2)}) collective-permute-start(f32[1,32,1024]{2,1,0:T(8,128)S(1)} %multiply_add_fusion), channel_id=1, source_target_pairs={{0,32},{32,64},{64,96},{96,128},{128,160},{160,192},{192,224},{224... | collective-permute-start | bytes 393224 | tf_op jit(solution)/shard_map/ppermute | solution.py:18
  1491.1 78.5 %collective-permute-start.17 = (f32[1,32,1024]{2,1,0:T(8,128)S(1)}, f32[1,32,1024]{2,1,0:T(8,128)S(1)}, u32[]{:S(2)}, u32[]{:S(2)}) collective-permute-start(f32[1,32,1024]{2,1,0:T(8,128)S(1)} %multiply_add_fusion.2), channel_id=1, source_target_pairs={{32,0},{64,32},{96,64},{128,96},{160,128},{192,160},{224,192},{256... | collective-permute-start | bytes 393224 | tf_op jit(solution)/shard_map/ppermute | solution.py:19
  1495.5 76.1 %collective-permute-start.16 = (f32[1,32,1024]{2,1,0:T(8,128)S(1)}, f32[1,32,1024]{2,1,0:T(8,128)S(1)}, u32[]{:S(2)}, u32[]{:S(2)}) collective-permute-start(f32[1,32,1024]{2,1,0:T(8,128)S(1)} %multiply_add_fusion.2), channel_id=1, source_target_pairs={{0,32},{32,64},{64,96},{96,128},{128,160},{160,192},{192,224},{224... | collective-permute-start | bytes 393224 | tf_op jit(solution)/shard_map/ppermute | solution.py:18
  1527.5 45.1 %collective-permute-start.15 = (f32[1,32,1024]{2,1,0:T(8,128)S(1)}, f32[1,32,1024]{2,1,0:T(8,128)S(1)}, u32[]{:S(2)}, u32[]{:S(2)}) collective-permute-start(f32[1,32,1024]{2,1,0:T(8,128)S(1)} %multiply_add_fusion.4), channel_id=1, source_target_pairs={{32,0},{64,32},{96,64},{128,96},{160,128},{192,160},{224,192},{256... | collective-permute-start | bytes 393224 | tf_op jit(solution)/shard_map/ppermute | solution.py:19
  1562.8 9.8 collective-permute-start.14
  1564.8 8.4 collective-permute-start.13
  1569.7 7.5 collective-permute-start.12
where the time goes:
time: 1610 us; the launch traced here: 1590 us
  other arithmetic  1080 us (67%)
  starting transfers between devices  370 us (23%)
  local copies, waits for them, and re-layouts  106 us (7%)
  waiting for transfers between devices  27.5 us (2%)
    add x26, other arithmetic, shifted_sum(): summed + kernel[position] * lax.slice_in_dim(padded, offset, offset + len...  722 us
    div x8, other arithmetic, shards(): quotient = observed_turned[view_at].reshape(planes, -1) / flattened  274 us
    all_to_all x8, starting transfers between devices, shards(): lax.all_to_all(returned, 'lane', split_axis=1, concat_axis=2, tiled=True)  138 us
    all_to_all x8, starting transfers between devices, shards(): lax.all_to_all(blurred, 'lane', split_axis=2, concat_axis=1, tiled=True)  138 us
    ppermute x10, starting transfers between devices, with_halo(): after = lax.ppermute(first, axis, down)  36.6 us
    unnamed x55, local copies, waits for them, and re-layouts  33.3 us
  transfers between devices with their start and end apart: 39, of which 4 were waited for; matrix products, arithmetic and copies ran while one was open for 66% of the time, Pallas kernels for 0%

commit v1 on v0

v1 whole, which is shorter than its diff:
```python
import functools

import jax
import jax.numpy as jnp
from jax import lax
from jax.experimental import pallas as pl
from jax.experimental.pallas import tpu as pltpu
from jax.sharding import PartitionSpec as P

ITERS = 2
HALO = 24
MESH = pl.DeviceIdType.MESH
F32, BF16 = jnp.float32, jnp.bfloat16


def halves(x):
    high = x.astype(BF16)
    return high, (x - high.astype(F32)).astype(BF16)


def dot(a, b):
    return jnp.dot(a, b, preferred_element_type=F32)


def iota(shape, dim):
    return lax.broadcasted_iota(jnp.int32, shape, dim)


def total_of(ref, *at, size):
    summed = ref[(*at, 0)]
    for k in range(1, size):
        summed = summed + ref[(*at, k)]
    return summed


def along_y(x, taps):
    rows, width = x.shape
    blocks = width // 128
    padded = pltpu.roll(jnp.concatenate([x, jnp.zeros((rows, 128), F32)], axis=1), 64, 1)
    high, low = halves(padded)
    windows = [part[:, 128 * b : 128 * b + 256] for part in (high, low) for b in range(blocks)]
    r = dot(jnp.concatenate(windows, axis=0), taps)
    n = blocks * rows
    summed = r[:n, :128] + (r[:n, 128:] + r[n:, :128])
    return jnp.concatenate([summed[rows * b : rows * (b + 1)] for b in range(blocks)], axis=1)


def kernel(groups, lanes, views, cap, est, lines, codes, shift, psf_x, psf_yz, out,
           outgoing, arrived, meta_out, meta_in, cur, part, part_in, edge, edge_in,
           m_fwd, m_adj, m_adj_low, t_fwd, t_adj, observed, blurred, spread,
           send_sem, recv_sem, a2a_send, a2a_recv, meta_send, meta_recv):
    p, l = lax.axis_index("grp"), lax.axis_index("lane")
    depth, width = est.shape
    taps = psf_yz.shape[2]
    reach = (taps - 1) // 2
    slots = views * cap
    span = depth + 2 * HALO
    all_rows = views * depth
    chunk = min(256, width)
    has = {"before": p > 0, "after": p < groups - 1, "up": l > 0, "down": l < lanes - 1}
    where = {
        "before": (jnp.maximum(p - 1, 0), l),
        "after": (jnp.minimum(p + 1, groups - 1), l),
        "up": (p, jnp.maximum(l - 1, 0)),
        "down": (p, jnp.minimum(l + 1, lanes - 1)),
    }
    opposite = {"before": "after", "after": "before", "up": "down", "down": "up"}
    counter = [0]

    class Copy:
        def __init__(self, side, src, dst):
            at = counter[0]
            counter[0] += 1
            self.to, self.since = has[side], has[opposite[side]]
            self.copy = pltpu.make_async_remote_copy(
                src_ref=src, dst_ref=dst, send_sem=send_sem.at[at], recv_sem=recv_sem.at[at],
                device_id=where[side], device_id_type=MESH,
            )
            pl.when(self.to)(self.copy.start)

        def arrive(self):
            pl.when(self.since)(self.copy.wait_recv)

        def leave(self):
            pl.when(self.to)(self.copy.wait_send)

    for it in range(ITERS):
        cur[it, 3 * span :] = jnp.zeros((cur.shape[1] - 3 * span, width), F32)

    @pl.when(p == 0)
    def _():
        for it in range(ITERS):
            cur[it, 0:span] = jnp.zeros((span, width), F32)
            part_in[it, 0] = jnp.zeros((span, width), F32)

    @pl.when(p == groups - 1)
    def _():
        for it in range(ITERS):
            cur[it, 2 * span : 3 * span] = jnp.zeros((span, width), F32)
            part_in[it, 1] = jnp.zeros((span, width), F32)

    @pl.when(l == 0)
    def _():
        for it in range(ITERS):
            for plane in range(3):
                cur[it, plane * span : plane * span + HALO] = jnp.zeros((HALO, width), F32)
            edge_in[it, 0] = jnp.zeros((HALO, width), F32)

    @pl.when(l == lanes - 1)
    def _():
        for it in range(ITERS):
            for plane in range(3):
                cur[it, (plane + 1) * span - HALO : (plane + 1) * span] = jnp.zeros((HALO, width), F32)
            edge_in[it, 1] = jnp.zeros((HALO, width), F32)

    barrier = pltpu.get_barrier_semaphore()
    for k in range(1, groups):
        pl.semaphore_signal(barrier, inc=1, device_id=(lax.rem(p + k, groups), l), device_id_type=MESH)
    for side in ("up", "down"):

        @pl.when(has[side])
        def _(side=side):
            pl.semaphore_signal(barrier, inc=1, device_id=where[side], device_id_type=MESH)

    own = pl.ds(span + HALO, depth)
    cur[0, own] = est[...]

    n_lines = codes.shape[1]
    per_view = n_lines // views
    code = codes[...]
    owner, landing = code // depth, code % depth
    line_at = iota((1, n_lines), 1)
    view = line_at // per_view
    key = view * groups + owner
    wide = jnp.broadcast_to(key, (n_lines, n_lines))
    earlier = iota((n_lines, n_lines), 0) < iota((n_lines, n_lines), 1)
    same = jnp.where((wide == wide.T) & earlier, 1.0, 0.0)
    rank = jnp.sum(same, axis=0, keepdims=True).astype(jnp.int32)
    in_block = view * cap + rank
    picks = jnp.where(iota((groups * slots, n_lines), 0) == owner * slots + in_block, 1.0, 0.0).astype(BF16)
    named = jnp.where(iota((groups, n_lines), 0) == owner, view * depth + landing + 1, 0)
    place = jnp.where(iota((groups * slots, n_lines), 0) == p * slots + in_block, 1.0, 0.0).astype(BF16)
    meta = lax.dot_general(
        named.astype(F32).astype(BF16), place, (((1,), (1,)), ((), ())), preferred_element_type=F32
    )
    for g in range(groups):
        meta_out[g] = meta[g : g + 1]
    picks2 = jnp.concatenate([picks, picks], axis=1)
    for at in range(0, width, chunk):
        high, low = halves(lines[:, at : at + chunk])
        packed = dot(picks2, jnp.concatenate([high, low], axis=0))
        outgoing[:, :, at : at + chunk] = packed.reshape(groups, slots, chunk)

    pl.semaphore_wait(
        barrier, groups - 1 + jnp.where(has["up"], 1, 0) + jnp.where(has["down"], 1, 0)
    )

    def widen_start(it):
        now = cur.at[it]
        lo, hi = span, 2 * span
        ups = [
            Copy("up", now.at[lo + HALO : lo + 2 * HALO], now.at[hi - HALO : hi]),
            Copy("down", now.at[hi - 2 * HALO : hi - HALO], now.at[lo : lo + HALO]),
        ]
        own_rows = now.at[lo + HALO : hi - HALO]
        mids = [
            Copy("before", own_rows, now.at[2 * span + HALO : 3 * span - HALO]),
            Copy("after", own_rows, now.at[HALO : span - HALO]),
        ]
        return ups, mids

    def widen_finish(it, ups, mids):
        now = cur.at[it]
        for c, at in ((ups[1], 0), (ups[0], span - HALO)):
            c.arrive()
            got = now.at[span + at : span + at + HALO]
            mids.append(Copy("before", got, now.at[2 * span + at : 2 * span + at + HALO]))
            mids.append(Copy("after", got, now.at[at : at + HALO]))
        for c in mids:
            c.arrive()
        for c in ups + mids:
            c.leave()

    ups, mids = widen_start(0)
    routes = []
    for k in sorted(range(1, groups), key=lambda k: -min(k, groups - k)):
        to = (lax.rem(p + k, groups), l)
        for src, dst, sent, got in (
            (meta_out.at[to[0]], meta_in.at[p], meta_send, meta_recv),
            (outgoing.at[to[0]], arrived.at[p], a2a_send, a2a_recv),
        ):
            c = pltpu.make_async_remote_copy(
                src_ref=src, dst_ref=dst, send_sem=sent.at[k], recv_sem=got.at[k],
                device_id=to, device_id_type=MESH,
            )
            c.start()
            routes.append(c)
    arrived[p] = outgoing[p]
    meta_in[p] = meta_out[p]

    columns = m_fwd.shape[1]
    column = iota((depth, columns), 1)
    plane = jnp.where(column < span, 0, jnp.where(column < 2 * span, 1, 2))
    tap_at = iota((depth, columns), 0) + (reach + HALO) - (column - plane * span)
    tap_at = jnp.where(column < 3 * span, tap_at, -1)
    blocks = []
    for v in range(views):
        acc = jnp.zeros((depth, columns), F32)
        for t in range(taps):
            acc = jnp.where(tap_at == t, psf_yz[v, 1, t], acc)
        across = jnp.where(plane == 0, psf_x[v, 2], jnp.where(plane == 1, psf_x[v, 1], psf_x[v, 0]))
        norm = jnp.full((1, columns), total_of(psf_yz, v, 1, size=taps)) * jnp.full(
            (1, columns), total_of(psf_x, v, size=3)
        )
        blocks.append(acc * across / norm)
    matrix = jnp.concatenate(blocks, axis=0)
    high, low = halves(matrix)
    m_fwd[0:all_rows] = high
    m_fwd[all_rows:] = low
    high, low = halves(matrix.T)
    m_adj[:, 0:all_rows] = high
    m_adj[:, all_rows:] = high
    m_adj_low[...] = low

    rows = 32

    def band(step, carry):
        i = iota((rows, 128), 0) + step * rows
        j = iota((rows, 128), 1)
        for v in range(views):
            norm = jnp.full((1, 128), total_of(psf_yz, v, 0, size=taps))
            for ref, at in ((t_fwd, j - i + (64 + reach + shift[v])), (t_adj, i - j + (reach - 64 + shift[v]))):
                acc = jnp.zeros((rows, 128), F32)
                for t in range(taps):
                    acc = jnp.where(at == t, psf_yz[v, 0, t], acc)
                high, low = halves(acc / norm)
                ref[v, pl.ds(pl.multiple_of(step * rows, rows), rows), 0:128] = high
                ref[v, pl.ds(pl.multiple_of(step * rows, rows), rows), 128:256] = low
        return carry

    lax.fori_loop(0, 256 // rows, band, 0)

    def blur(it):
        for at in range(0, width, chunk):
            high, low = halves(cur[it, :, at : at + chunk])
            r = dot(m_fwd[...], high)
            spread[:, at : at + chunk] = r[:all_rows] + (r[all_rows:] + dot(m_fwd[0:all_rows], low))
        for v in range(views):
            blurred[v * depth : (v + 1) * depth] = along_y(spread[v * depth : (v + 1) * depth], t_fwd[v])

    widen_finish(0, ups, mids)
    blur(0)

    for c in routes:
        c.wait()
    marks = jnp.sum(meta_in[...], axis=0)
    lands = jnp.where(iota((all_rows, groups * slots), 0) + 1 == marks.astype(jnp.int32), 1.0, 0.0).astype(BF16)
    for at in range(0, width, chunk):
        high, low = halves(arrived[:, :, at : at + chunk].reshape(groups * slots, chunk))
        observed[:, at : at + chunk] = dot(lands, high) + dot(lands, low)

    for it in range(ITERS):
        if it > 0:
            widen_finish(it, *widen_start(it))
            blur(it)
        y = iota((depth, width), 1)
        for v in range(views):
            at = pl.ds(v * depth, depth)
            seen = y + shift[v]
            quotient = jnp.where((seen >= 0) & (seen < width), observed[at] / blurred[at], 0.0)
            spread[at] = along_y(quotient, t_adj[v])
        for at in range(0, width, chunk):
            high, low = halves(spread[:, at : at + chunk])
            r = dot(m_adj[...], jnp.concatenate([high, low], axis=0)) + dot(m_adj_low[...], high)
            part[it, :, at : at + chunk] = r
        mine, theirs = part.at[it], part_in.at[it]
        shares = []
        for rows_at in ((0, HALO), (span - HALO, span), (HALO, span - HALO)):
            a, b = rows_at
            shares.append([
                Copy("before", mine.at[a:b], theirs.at[1, a:b]),
                Copy("after", mine.at[2 * span + a : 2 * span + b], theirs.at[0, a:b]),
            ])
        edges = []
        for n, (side, a) in enumerate((("up", 0), ("down", span - HALO))):
            for c in shares[n]:
                c.arrive()
            rows_at = pl.ds(a, HALO)
            edge[it, n] = part[it, pl.ds(span + a, HALO)] + (part_in[it, 0, rows_at] + part_in[it, 1, rows_at])
            edges.append(Copy(side, edge.at[it, n], edge_in.at[it, 1 - n]))
        for c in shares[2]:
            c.arrive()
        mid = pl.ds(HALO, depth)
        correction = part[it, own] + (part_in[it, 0, mid] + part_in[it, 1, mid])
        for c in edges:
            c.arrive()
        rest = jnp.zeros((depth - HALO, width), F32)
        correction = correction + jnp.concatenate([edge_in[it, 0], rest], axis=0)
        correction = correction + jnp.concatenate([rest, edge_in[it, 1]], axis=0)
        new = cur[it, own] * correction * (1.0 / views)
        if it + 1 < ITERS:
            cur[it + 1, own] = new
        else:
            out[...] = new
        for c in shares[0] + shares[1] + shares[2] + edges:
            c.leave()


def shards(groups, lanes, estimate, view_lines, line_owner, line_target, view_shift, psf_x, psf_yz):
    _, depth, width = estimate.shape
    views, n, _ = view_lines.shape
    cap = 2 * n // groups
    slots, span, all_rows = views * cap, depth + 2 * HALO, views * depth
    codes = (line_owner[:, :, 0] * depth + line_target).reshape(1, views * n)
    vmem, smem = pl.BlockSpec(memory_space=pltpu.VMEM), pl.BlockSpec(memory_space=pltpu.SMEM)
    columns = -(-3 * span // 128) * 128
    copies = 18 * ITERS
    out = pl.pallas_call(
        functools.partial(kernel, groups, lanes, views, cap),
        out_shape=jax.ShapeDtypeStruct((depth, width), F32),
        in_specs=[vmem, vmem, vmem, smem, smem, smem],
        out_specs=vmem,
        scratch_shapes=[
            pltpu.VMEM((groups, slots, width), F32),
            pltpu.VMEM((groups, slots, width), F32),
            pltpu.VMEM((groups, 1, groups * slots), F32),
            pltpu.VMEM((groups, 1, groups * slots), F32),
            pltpu.VMEM((ITERS, columns, width), F32),
            pltpu.VMEM((ITERS, columns, width), F32),
            pltpu.VMEM((ITERS, 2, span, width), F32),
            pltpu.VMEM((ITERS, 2, HALO, width), F32),
            pltpu.VMEM((ITERS, 2, HALO, width), F32),
            pltpu.VMEM((2 * all_rows, columns), BF16),
            pltpu.VMEM((columns, 2 * all_rows), BF16),
            pltpu.VMEM((columns, all_rows), BF16),
            pltpu.VMEM((views, 256, 256), BF16),
            pltpu.VMEM((views, 256, 256), BF16),
            pltpu.VMEM((all_rows, width), F32),
            pltpu.VMEM((all_rows, width), F32),
            pltpu.VMEM((all_rows, width), F32),
            pltpu.SemaphoreType.DMA((copies,)),
            pltpu.SemaphoreType.DMA((copies,)),
            pltpu.SemaphoreType.DMA((groups,)),
            pltpu.SemaphoreType.DMA((groups,)),
            pltpu.SemaphoreType.DMA((groups,)),
            pltpu.SemaphoreType.DMA((groups,)),
        ],
        compiler_params=pltpu.CompilerParams(
            collective_id=0, has_side_effects=True, vmem_limit_bytes=40 << 20
        ),
    )(
        estimate.reshape(depth, width),
        view_lines.reshape(views * n, width),
        codes,
        view_shift,
        psf_x,
        psf_yz,
    )
    return out.reshape(estimate.shape)


def solution(mesh):
    placed = (
        P("grp", "lane", None),
        P(None, ("grp", "lane"), None),
        P(None, ("grp", "lane"), None),
        P(None, ("grp", "lane")),
        P(),
        P(),
        P(),
    )
    return jax.shard_map(
        functools.partial(shards, mesh.shape["grp"], mesh.shape["lane"]),
        mesh=mesh, in_specs=placed, out_specs=P("grp", "lane", None), check_vma=False,
    )
```

time: 1610 us -> 124 us (0.08)
  the two profiles are of different devices: /device:TPU:398 before, /device:TPU:352 now
where the time goes in v1:
time: 124 us
  Pallas kernels  119 us (96%)
  local copies, waits for them, and re-layouts  4.65 us (4%)
    pallas_call x1, Pallas kernels, shards(): pl.pallas_call(functools.partial(kernel, groups, lanes, views, cap), out_...  119 us
    unnamed x15, local copies, waits for them, and re-layouts  4.57 us

profile of v1, /device:TPU:352, one launch (start us, length us, event | category | flops | bytes accessed | tf_op | source)
XLA Modules:
  0.0 124.0 jit_solution(15838913413338063530)
XLA Ops:
  0.0 0.0 copy-start.6
  0.0 0.7 copy-done.6
  0.7 0.0 copy-start.5
  0.7 0.7 copy-done.5
  1.4 0.0 copy-start.2
  1.4 0.0 copy-start.3
  1.4 0.0 copy-start.4
  1.4 0.1 reshape.16.codes
  1.5 0.6 copy-done.2
  2.1 0.0 copy-done.3
  2.1 0.0 copy-done.4
  2.1 0.0 copy-start
  2.1 1.0 copy-done
  3.1 0.0 copy-start.1
  3.1 0.9 copy-done.1
  4.0 119.4 %shard_map.73 = f32[32,1024]{1,0:T(8,128)S(1)} custom-call(f32[32,1024]{1,0:T(8,128)S(1)} %bitcast.6, f32[128,1024]{1,0:T(8,128)S(1)} %bitcast.5, s32[1,128]{1,0:T(1,128)S(1)} %reshape.16.codes, s32[4]{0:T(128)S(1)} %copy-done.4, f32[4,3]{1,0:T(4,128)S(1)} %copy-done.3, f32[4,2,41]{2,1,0:T(2,128)S(1)} %copy-done.2), custom_call_target="tpu_custom_call" | custom-call | tf_op jit(solution)/shard_map/pallas_call | solution.py:318
  123.4 0.7 copy.9
  (2 shorter events, 0.0 us)
Async XLA Ops:
  0.0 0.7 copy-start.6
  0.7 0.7 copy-start.5
  1.4 0.7 copy-start.2
  1.4 0.7 copy-start.3
  1.4 0.7 copy-start.4
  2.1 1.0 copy-start
  3.1 0.9 copy-start.1

commit v2 on v1

--- a/solution.py
+++ b/solution.py
@@ -45,12 +45,13 @@
     return jnp.concatenate([summed[rows * b : rows * (b + 1)] for b in range(blocks)], axis=1)
 
 
-def kernel(groups, lanes, views, cap, est, lines, codes, shift, psf_x, psf_yz, out,
-           outgoing, arrived, meta_out, meta_in, cur, part, part_in, edge, edge_in,
+def kernel(groups, lanes, views, cap, est_at, lines_at, owner_at, target_at, shift_at, psf_x_at, psf_yz_at, out,
+           lines, owners, targets, shift, psf_x, psf_yz, load_sem,
+           outgoing, arrived, meta_out, meta_in, cur, part, part_in, edge, edge_in, beyond, passing,
            m_fwd, m_adj, m_adj_low, t_fwd, t_adj, observed, blurred, spread,
            send_sem, recv_sem, a2a_send, a2a_recv, meta_send, meta_recv):
     p, l = lax.axis_index("grp"), lax.axis_index("lane")
-    depth, width = est.shape
+    depth, width = est_at.shape
     taps = psf_yz.shape[2]
     reach = (taps - 1) // 2
     slots = views * cap
@@ -68,13 +69,13 @@
     counter = [0]
 
     class Copy:
-        def __init__(self, side, src, dst):
+        def __init__(self, to, since, target, src, dst):
             at = counter[0]
             counter[0] += 1
-            self.to, self.since = has[side], has[opposite[side]]
+            self.to, self.since = to, since
             self.copy = pltpu.make_async_remote_copy(
                 src_ref=src, dst_ref=dst, send_sem=send_sem.at[at], recv_sem=recv_sem.at[at],
-                device_id=where[side], device_id_type=MESH,
+                device_id=target, device_id_type=MESH,
             )
             pl.when(self.to)(self.copy.start)
 
@@ -83,6 +84,43 @@
 
         def leave(self):
             pl.when(self.to)(self.copy.wait_send)
+
+    def beside(side, src, dst):
+        return Copy(has[side], has[opposite[side]], where[side], src, dst)
+
+    high_lane = lanes // 2
+    low_lane = high_lane - 1
+    far_low, far_high = high_lane - 4, high_lane + 3
+    near = {"up": has["up"] & (l != high_lane), "down": has["down"] & (l != low_lane)}
+
+    def between(a, b, src, dst):
+        return Copy(l == a, l == b, (p, jnp.int32(b)), src, dst)
+
+    barrier = pltpu.get_barrier_semaphore()
+    for k in range(1, groups):
+        pl.semaphore_signal(barrier, inc=1, device_id=(lax.rem(p + k, groups), l), device_id_type=MESH)
+    expected = groups - 1
+    greeted = [(has[side], where[side]) for side in ("up", "down")]
+    for a, b in ((far_low, low_lane), (far_low, high_lane), (low_lane - 1, high_lane),
+                 (far_high, high_lane), (far_high, low_lane), (high_lane + 1, low_lane)):
+        greeted += [(l == a, (p, jnp.int32(b))), (l == b, (p, jnp.int32(a)))]
+    for cond, device in greeted:
+        expected = expected + jnp.where(cond, 1, 0)
+
+        @pl.when(cond)
+        def _(device=device):
+            pl.semaphore_signal(barrier, inc=1, device_id=device, device_id_type=MESH)
+
+    own = pl.ds(span + HALO, depth)
+    loads = [
+        pltpu.make_async_copy(src, dst, load_sem.at[n])
+        for n, (src, dst) in enumerate((
+            (owner_at, owners), (target_at, targets), (lines_at, lines), (est_at, cur.at[0, own]),
+            (shift_at, shift), (psf_x_at, psf_x), (psf_yz_at, psf_yz),
+        ))
+    ]
+    for c in loads:
+        c.start()
 
     for it in range(ITERS):
         cur[it, 3 * span :] = jnp.zeros((cur.shape[1] - 3 * span, width), F32)
@@ -102,33 +140,22 @@
     @pl.when(l == 0)
     def _():
         for it in range(ITERS):
-            for plane in range(3):
-                cur[it, plane * span : plane * span + HALO] = jnp.zeros((HALO, width), F32)
+            cur[it, span : span + HALO] = jnp.zeros((HALO, width), F32)
             edge_in[it, 0] = jnp.zeros((HALO, width), F32)
 
     @pl.when(l == lanes - 1)
     def _():
         for it in range(ITERS):
-            for plane in range(3):
-                cur[it, (plane + 1) * span - HALO : (plane + 1) * span] = jnp.zeros((HALO, width), F32)
+            cur[it, 2 * span - HALO : 2 * span] = jnp.zeros((HALO, width), F32)
             edge_in[it, 1] = jnp.zeros((HALO, width), F32)
 
-    barrier = pltpu.get_barrier_semaphore()
-    for k in range(1, groups):
-        pl.semaphore_signal(barrier, inc=1, device_id=(lax.rem(p + k, groups), l), device_id_type=MESH)
-    for side in ("up", "down"):
-
-        @pl.when(has[side])
-        def _(side=side):
-            pl.semaphore_signal(barrier, inc=1, device_id=where[side], device_id_type=MESH)
-
-    own = pl.ds(span + HALO, depth)
-    cur[0, own] = est[...]
-
-    n_lines = codes.shape[1]
+    for c in loads:
+        c.wait()
+
+    n_lines = lines.shape[0]
     per_view = n_lines // views
-    code = codes[...]
-    owner, landing = code // depth, code % depth
+    owner = jnp.concatenate([owners[v : v + 1, :] for v in range(views)], axis=1)
+    landing = jnp.concatenate([targets[v : v + 1, :] for v in range(views)], axis=1)
     line_at = iota((1, n_lines), 1)
     view = line_at // per_view
     key = view * groups + owner
@@ -151,21 +178,22 @@
         packed = dot(picks2, jnp.concatenate([high, low], axis=0))
         outgoing[:, :, at : at + chunk] = packed.reshape(groups, slots, chunk)
 
-    pl.semaphore_wait(
-        barrier, groups - 1 + jnp.where(has["up"], 1, 0) + jnp.where(has["down"], 1, 0)
-    )
+    pl.semaphore_wait(barrier, expected)
+
+    departed = []
 
     def widen_start(it):
         now = cur.at[it]
         lo, hi = span, 2 * span
+        sides = near if it > 0 else has
         ups = [
-            Copy("up", now.at[lo + HALO : lo + 2 * HALO], now.at[hi - HALO : hi]),
-            Copy("down", now.at[hi - 2 * HALO : hi - HALO], now.at[lo : lo + HALO]),
+            Copy(sides["up"], sides["down"], where["up"], now.at[lo + HALO : lo + 2 * HALO], now.at[hi - HALO : hi]),
+            Copy(sides["down"], sides["up"], where["down"], now.at[hi - 2 * HALO : hi - HALO], now.at[lo : lo + HALO]),
         ]
         own_rows = now.at[lo + HALO : hi - HALO]
         mids = [
-            Copy("before", own_rows, now.at[2 * span + HALO : 3 * span - HALO]),
-            Copy("after", own_rows, now.at[HALO : span - HALO]),
+            beside("before", own_rows, now.at[2 * span + HALO : 3 * span - HALO]),
+            beside("after", own_rows, now.at[HALO : span - HALO]),
         ]
         return ups, mids
 
@@ -174,12 +202,11 @@
         for c, at in ((ups[1], 0), (ups[0], span - HALO)):
             c.arrive()
             got = now.at[span + at : span + at + HALO]
-            mids.append(Copy("before", got, now.at[2 * span + at : 2 * span + at + HALO]))
-            mids.append(Copy("after", got, now.at[at : at + HALO]))
+            mids.append(beside("before", got, now.at[2 * span + at : 2 * span + at + HALO]))
+            mids.append(beside("after", got, now.at[at : at + HALO]))
         for c in mids:
             c.arrive()
-        for c in ups + mids:
-            c.leave()
+        departed.extend(ups + mids)
 
     ups, mids = widen_start(0)
     routes = []
@@ -278,20 +305,34 @@
         for rows_at in ((0, HALO), (span - HALO, span), (HALO, span - HALO)):
             a, b = rows_at
             shares.append([
-                Copy("before", mine.at[a:b], theirs.at[1, a:b]),
-                Copy("after", mine.at[2 * span + a : 2 * span + b], theirs.at[0, a:b]),
+                beside("before", mine.at[a:b], theirs.at[1, a:b]),
+                beside("after", mine.at[2 * span + a : 2 * span + b], theirs.at[0, a:b]),
             ])
-        edges = []
+        edges, across = [], []
         for n, (side, a) in enumerate((("up", 0), ("down", span - HALO))):
             for c in shares[n]:
                 c.arrive()
             rows_at = pl.ds(a, HALO)
             edge[it, n] = part[it, pl.ds(span + a, HALO)] + (part_in[it, 0, rows_at] + part_in[it, 1, rows_at])
-            edges.append(Copy(side, edge.at[it, n], edge_in.at[it, 1 - n]))
+            edges.append(beside(side, edge.at[it, n], edge_in.at[it, 1 - n]))
+        if it + 1 < ITERS:
+            across += [
+                between(low_lane - 1, high_lane, edge.at[it, 1], beyond.at[0]),
+                between(high_lane + 1, low_lane, edge.at[it, 0], beyond.at[0]),
+            ]
         for c in shares[2]:
             c.arrive()
         mid = pl.ds(HALO, depth)
         correction = part[it, own] + (part_in[it, 0, mid] + part_in[it, 1, mid])
+        if it + 1 < ITERS:
+            passing[0] = correction
+            first = [
+                between(low_lane, far_low, passing.at[0, depth - HALO :], passing.at[1, 0:HALO]),
+                between(high_lane, far_high, passing.at[0, 0:HALO], passing.at[1, 0:HALO]),
+            ]
+            for c, a, b in ((first[0], far_low, high_lane), (first[1], far_high, low_lane)):
+                c.arrive()
+                across.append(between(a, b, passing.at[1, 0:HALO], beyond.at[1]))
         for c in edges:
             c.arrive()
         rest = jnp.zeros((depth - HALO, width), F32)
@@ -300,10 +341,30 @@
         new = cur[it, own] * correction * (1.0 / views)
         if it + 1 < ITERS:
             cur[it + 1, own] = new
+            for c in across:
+                c.arrive()
+            overlap = 2 * HALO - depth
+            blank = jnp.zeros((depth - HALO, width), F32)
+            for me, n, a in ((high_lane, 0, 0), (low_lane, 1, span - HALO)):
+
+                @pl.when(l == me)
+                def _(n=n, a=a, it=it):
+                    got = beyond[0]
+                    kept = (
+                        jnp.concatenate([got[HALO - overlap :], blank], axis=0)
+                        if n == 0
+                        else jnp.concatenate([blank, got[:overlap]], axis=0)
+                    )
+                    total = edge[it, n] + (beyond[1] + kept)
+                    rows_at = pl.ds(span + a, HALO)
+                    cur[it + 1, rows_at] = cur[it, rows_at] * total * (1.0 / views)
+
+            departed.extend(first + across)
         else:
             out[...] = new
-        for c in shares[0] + shares[1] + shares[2] + edges:
-            c.leave()
+        departed.extend(shares[0] + shares[1] + shares[2] + edges)
+    for c in departed:
+        c.leave()
 
 
 def shards(groups, lanes, estimate, view_lines, line_owner, line_target, view_shift, psf_x, psf_yz):
@@ -311,47 +372,58 @@
     views, n, _ = view_lines.shape
     cap = 2 * n // groups
     slots, span, all_rows = views * cap, depth + 2 * HALO, views * depth
-    codes = (line_owner[:, :, 0] * depth + line_target).reshape(1, views * n)
-    vmem, smem = pl.BlockSpec(memory_space=pltpu.VMEM), pl.BlockSpec(memory_space=pltpu.SMEM)
+    hbm = pl.BlockSpec(memory_space=pltpu.HBM)
     columns = -(-3 * span // 128) * 128
-    copies = 18 * ITERS
+    copies = 18 * ITERS + 6
+    vmem = lambda *shape: pltpu.VMEM(shape, F32)
+    dma = lambda n: pltpu.SemaphoreType.DMA((n,))
     out = pl.pallas_call(
         functools.partial(kernel, groups, lanes, views, cap),
         out_shape=jax.ShapeDtypeStruct((depth, width), F32),
-        in_specs=[vmem, vmem, vmem, smem, smem, smem],
-        out_specs=vmem,
+        in_specs=[hbm] * 7,
+        out_specs=pl.BlockSpec(memory_space=pltpu.VMEM),
         scratch_shapes=[
-            pltpu.VMEM((groups, slots, width), F32),
-            pltpu.VMEM((groups, slots, width), F32),
-            pltpu.VMEM((groups, 1, groups * slots), F32),
-            pltpu.VMEM((groups, 1, groups * slots), F32),
-            pltpu.VMEM((ITERS, columns, width), F32),
-            pltpu.VMEM((ITERS, columns, width), F32),
-            pltpu.VMEM((ITERS, 2, span, width), F32),
-            pltpu.VMEM((ITERS, 2, HALO, width), F32),
-            pltpu.VMEM((ITERS, 2, HALO, width), F32),
+            vmem(views * n, width),
+            pltpu.VMEM((views, n), jnp.int32),
+            pltpu.VMEM((views, n), jnp.int32),
+            pltpu.SMEM(view_shift.shape, jnp.int32),
+            pltpu.SMEM(psf_x.shape, F32),
+            pltpu.SMEM(psf_yz.shape, F32),
+            dma(7),
+            vmem(groups, slots, width),
+            vmem(groups, slots, width),
+            vmem(groups, 1, groups * slots),
+            vmem(groups, 1, groups * slots),
+            vmem(ITERS, columns, width),
+            vmem(ITERS, columns, width),
+            vmem(ITERS, 2, span, width),
+            vmem(ITERS, 2, HALO, width),
+            vmem(ITERS, 2, HALO, width),
+            vmem(2, HALO, width),
+            vmem(2, depth, width),
             pltpu.VMEM((2 * all_rows, columns), BF16),
             pltpu.VMEM((columns, 2 * all_rows), BF16),
             pltpu.VMEM((columns, all_rows), BF16),
             pltpu.VMEM((views, 256, 256), BF16),
             pltpu.VMEM((views, 256, 256), BF16),
-            pltpu.VMEM((all_rows, width), F32),
-            pltpu.VMEM((all_rows, width), F32),
-            pltpu.VMEM((all_rows, width), F32),
-            pltpu.SemaphoreType.DMA((copies,)),
-            pltpu.SemaphoreType.DMA((copies,)),
-            pltpu.SemaphoreType.DMA((groups,)),
-            pltpu.SemaphoreType.DMA((groups,)),
-            pltpu.SemaphoreType.DMA((groups,)),
-            pltpu.SemaphoreType.DMA((groups,)),
+            vmem(all_rows, width),
+            vmem(all_rows, width),
+            vmem(all_rows, width),
+            dma(copies),
+            dma(copies),
+            dma(groups),
+            dma(groups),
+            dma(groups),
+            dma(groups),
         ],
         compiler_params=pltpu.CompilerParams(
-            collective_id=0, has_side_effects=True, vmem_limit_bytes=40 << 20
+            collective_id=0, has_side_effects=True, vmem_limit_bytes=64 << 20
         ),
     )(
         estimate.reshape(depth, width),
         view_lines.reshape(views * n, width),
-        codes,
+        line_owner[:, :, 0],
+        line_target,
         view_shift,
         psf_x,
         psf_yz,

time: 124 us -> 119 us (0.960)
  the two profiles are of different devices: /device:TPU:352 before, /device:TPU:127 now
where the time goes in v2:
time: 119 us
  Pallas kernels  117 us (98%)
  local copies, waits for them, and re-layouts  1.57 us (1%)
    pallas_call x1, Pallas kernels, shards(): pl.pallas_call(functools.partial(kernel, groups, lanes, views, cap), out_...  117 us

profile of v2, /device:TPU:127, one launch (start us, length us, event | category | flops | bytes accessed | tf_op | source)
XLA Modules:
  0.0 118.6 jit_solution(15191706378004455816)
XLA Ops:
  0.0 117.0 %shard_map.73 = f32[32,1024]{1,0:T(8,128)} custom-call(f32[32,1024]{1,0:T(8,128)} %bitcast.6, f32[128,1024]{1,0:T(8,128)} %bitcast.4, s32[4,32]{1,0:T(4,128)} %bitcast.7, s32[4,32]{1,0:T(4,128)} %target_at.1, s32[4]{0:T(128)} %shift_at.1, f32[4,3]{1,0:T(4,128)} %psf_x_at.1, f32[4,2,41]{2,1,0:T(2,128)} %psf_yz_at.1), custom_call_target="tpu_custom_call" | custom-call | tf_op jit(solution)/shard_map/pallas_call | solution.py:380
  117.0 1.6 %copy.9 = f32[1,32,1024]{2,1,0:T(8,128)} copy(f32[1,32,1024]{2,1,0:T(8,128)} %bitcast.5) | data formatting | bytes 262144

commit v3 on v2

--- a/solution.py
+++ b/solution.py
@@ -8,6 +8,7 @@
 from jax.sharding import PartitionSpec as P
 
 ITERS = 2
+AHEAD = 1
 HALO = 24
 MESH = pl.DeviceIdType.MESH
 F32, BF16 = jnp.float32, jnp.bfloat16
@@ -45,11 +46,19 @@
     return jnp.concatenate([summed[rows * b : rows * (b + 1)] for b in range(blocks)], axis=1)
 
 
+def relays(groups, lanes):
+    middle = groups // 2
+    if lanes < 32 or groups < 8:
+        return [(0, middle)], lanes // 2 - 1
+    plan = [(0, middle+0), (0, middle-1), (0, middle+1), (0, middle+2), (1, middle+0)]
+    return plan, lanes // 2 - 6
+
+
 def kernel(groups, lanes, views, cap, est_at, lines_at, owner_at, target_at, shift_at, psf_x_at, psf_yz_at, out,
            lines, owners, targets, shift, psf_x, psf_yz, load_sem,
-           outgoing, arrived, meta_out, meta_in, cur, part, part_in, edge, edge_in, beyond, passing,
+           outgoing, arrived, meta_out, meta_in, cur, part, part_in, edge, edge_in, beyond, passing, relayed,
            m_fwd, m_adj, m_adj_low, t_fwd, t_adj, observed, blurred, spread,
-           send_sem, recv_sem, a2a_send, a2a_recv, meta_send, meta_recv):
+           send_sem, recv_sem, relay_send, a2a_send, a2a_recv, meta_send, meta_recv):
     p, l = lax.axis_index("grp"), lax.axis_index("lane")
     depth, width = est_at.shape
     taps = psf_yz.shape[2]
@@ -96,6 +105,16 @@
     def between(a, b, src, dst):
         return Copy(l == a, l == b, (p, jnp.int32(b)), src, dst)
 
+    half = lanes // 2
+    from_end = jnp.minimum(l, lanes - 1 - l)
+    plan, pool = relays(groups, lanes)
+
+    def in_half(lane):
+        return jnp.where(l < half, lane, lanes - 1 - lane)
+
+    def relay_of(plane, n):
+        return lax.rem(len(plan) * plane + n, pool)
+
     barrier = pltpu.get_barrier_semaphore()
     for k in range(1, groups):
         pl.semaphore_signal(barrier, inc=1, device_id=(lax.rem(p + k, groups), l), device_id_type=MESH)
@@ -104,8 +123,16 @@
     for a, b in ((far_low, low_lane), (far_low, high_lane), (low_lane - 1, high_lane),
                  (far_high, high_lane), (far_high, low_lane), (high_lane + 1, low_lane)):
         greeted += [(l == a, (p, jnp.int32(b))), (l == b, (p, jnp.int32(a)))]
+    for cond, _ in greeted:
+        expected = expected + jnp.where(cond, 1, 0)
+    for n, (distance, k) in enumerate(plan):
+        source = half - 1 - distance
+        is_source, is_relay = from_end == source, from_end == relay_of(p, n)
+        expected = expected + jnp.where(is_source, 1, 0) + jnp.where(is_relay, 1, 0)
+        sender = lax.rem(p + groups - k, groups)
+        greeted.append((is_relay, (p, in_half(source))))
+        greeted.append((is_source, (sender, in_half(relay_of(sender, n)))))
     for cond, device in greeted:
-        expected = expected + jnp.where(cond, 1, 0)
 
         @pl.when(cond)
         def _(device=device):
@@ -180,8 +207,6 @@
 
     pl.semaphore_wait(barrier, expected)
 
-    departed = []
-
     def widen_start(it):
         now = cur.at[it]
         lo, hi = span, 2 * span
@@ -208,20 +233,50 @@
             c.arrive()
         departed.extend(ups + mids)
 
+    departed = []
+    first_legs = [
+        Copy(
+            from_end == half - 1 - distance, from_end == relay_of(p, n), (p, in_half(relay_of(p, n))),
+            outgoing.at[lax.rem(p + k, groups)], relayed.at[n],
+        )
+        for n, (distance, k) in enumerate(plan)
+    ]
     ups, mids = widen_start(0)
     routes = []
-    for k in sorted(range(1, groups), key=lambda k: -min(k, groups - k)):
+
+    def pass_on():
+        for n, (distance, k) in enumerate(plan):
+            first_legs[n].arrive()
+            second = pltpu.make_async_remote_copy(
+                src_ref=relayed.at[n], dst_ref=arrived.at[p], send_sem=relay_send.at[n], recv_sem=a2a_recv.at[k],
+                device_id=(lax.rem(p + k, groups), in_half(half - 1 - distance)), device_id_type=MESH,
+            )
+            is_relay = from_end == relay_of(p, n)
+            pl.when(is_relay)(second.start)
+            routes.append((None, is_relay, second))
+
+    order = sorted(range(1, groups), key=lambda k: -min(k, groups - k))
+    for turn, k in enumerate(order):
+        if turn == AHEAD % len(order):
+            pass_on()
         to = (lax.rem(p + k, groups), l)
-        for src, dst, sent, got in (
-            (meta_out.at[to[0]], meta_in.at[p], meta_send, meta_recv),
-            (outgoing.at[to[0]], arrived.at[p], a2a_send, a2a_recv),
+        direct = p >= 0
+        for distance, offset in plan:
+            if offset == k:
+                direct = direct & (from_end != half - 1 - distance)
+        for always, src, dst, sent, got in (
+            (True, meta_out.at[to[0]], meta_in.at[p], meta_send, meta_recv),
+            (False, outgoing.at[to[0]], arrived.at[p], a2a_send, a2a_recv),
         ):
             c = pltpu.make_async_remote_copy(
                 src_ref=src, dst_ref=dst, send_sem=sent.at[k], recv_sem=got.at[k],
                 device_id=to, device_id_type=MESH,
             )
-            c.start()
-            routes.append(c)
+            if always:
+                c.start()
+            else:
+                pl.when(direct)(c.start)
+            routes.append((always, direct, c))
     arrived[p] = outgoing[p]
     meta_in[p] = meta_out[p]
 
@@ -278,8 +333,9 @@
     widen_finish(0, ups, mids)
     blur(0)
 
-    for c in routes:
-        c.wait()
+    for always, sent, c in routes:
+        if always is not None:
+            c.wait_recv()
     marks = jnp.sum(meta_in[...], axis=0)
     lands = jnp.where(iota((all_rows, groups * slots), 0) + 1 == marks.astype(jnp.int32), 1.0, 0.0).astype(BF16)
     for at in range(0, width, chunk):
@@ -363,7 +419,12 @@
         else:
             out[...] = new
         departed.extend(shares[0] + shares[1] + shares[2] + edges)
-    for c in departed:
+    for always, sent, c in routes:
+        if always:
+            c.wait_send()
+        else:
+            pl.when(sent)(c.wait_send)
+    for c in departed + first_legs:
         c.leave()
 
 
@@ -374,7 +435,8 @@
     slots, span, all_rows = views * cap, depth + 2 * HALO, views * depth
     hbm = pl.BlockSpec(memory_space=pltpu.HBM)
     columns = -(-3 * span // 128) * 128
-    copies = 18 * ITERS + 6
+    plan, _ = relays(groups, lanes)
+    copies = 18 * ITERS + 6 + len(plan)
     vmem = lambda *shape: pltpu.VMEM(shape, F32)
     dma = lambda n: pltpu.SemaphoreType.DMA((n,))
     out = pl.pallas_call(
@@ -401,6 +463,7 @@
             vmem(ITERS, 2, HALO, width),
             vmem(2, HALO, width),
             vmem(2, depth, width),
+            vmem(len(plan), slots, width),
             pltpu.VMEM((2 * all_rows, columns), BF16),
             pltpu.VMEM((columns, 2 * all_rows), BF16),
             pltpu.VMEM((columns, all_rows), BF16),
@@ -411,6 +474,7 @@
             vmem(all_rows, width),
             dma(copies),
             dma(copies),
+            dma(len(plan)),
             dma(groups),
             dma(groups),
             dma(groups),

time: 119 us -> 108 us (0.908)
  Pallas kernels: 117 us -> 106 us
    pallas_call x1, Pallas kernels: 117 us -> 106 us  [shards(): pl.pallas_call(functools.partial(kernel, groups, lanes, views, cap), out_...]
where the time goes in v3:
time: 108 us; the launch traced here: 107 us
  Pallas kernels  106 us (98%)
  local copies, waits for them, and re-layouts  1.57 us (1%)
    pallas_call x1, Pallas kernels, shards(): pl.pallas_call(functools.partial(kernel, groups, lanes, views, cap), out_...  106 us

profile of v3, /device:TPU:127, one launch (start us, length us, event | category | flops | bytes accessed | tf_op | source)
XLA Modules:
  0.0 107.4 jit_solution(7459775159856545456)
XLA Ops:
  0.0 105.8 %shard_map.73 = f32[32,1024]{1,0:T(8,128)} custom-call(f32[32,1024]{1,0:T(8,128)} %bitcast.6, f32[128,1024]{1,0:T(8,128)} %bitcast.4, s32[4,32]{1,0:T(4,128)} %bitcast.7, s32[4,32]{1,0:T(4,128)} %target_at.1, s32[4]{0:T(128)} %shift_at.1, f32[4,3]{1,0:T(4,128)} %psf_x_at.1, f32[4,2,41]{2,1,0:T(2,128)} %psf_yz_at.1), custom_call_target="tpu_custom_call" | custom-call | tf_op jit(solution)/shard_map/pallas_call | solution.py:442
  105.8 1.6 %copy.9 = f32[1,32,1024]{2,1,0:T(8,128)} copy(f32[1,32,1024]{2,1,0:T(8,128)} %bitcast.5) | data formatting | bytes 262144

commit v4 on v3

--- a/solution.py
+++ b/solution.py
@@ -8,6 +8,8 @@
 from jax.sharding import PartitionSpec as P
 
 ITERS = 2
+CORNERS = 9
+FAR_CORNERS = 12
 AHEAD = 1
 HALO = 24
 MESH = pl.DeviceIdType.MESH
@@ -78,7 +80,7 @@
     counter = [0]
 
     class Copy:
-        def __init__(self, to, since, target, src, dst):
+        def __init__(self, to, since, target, src, dst, now=True):
             at = counter[0]
             counter[0] += 1
             self.to, self.since = to, since
@@ -86,6 +88,10 @@
                 src_ref=src, dst_ref=dst, send_sem=send_sem.at[at], recv_sem=recv_sem.at[at],
                 device_id=target, device_id_type=MESH,
             )
+            if now:
+                self.start()
+
+        def start(self):
             pl.when(self.to)(self.copy.start)
 
         def arrive(self):
@@ -102,8 +108,8 @@
     far_low, far_high = high_lane - 4, high_lane + 3
     near = {"up": has["up"] & (l != high_lane), "down": has["down"] & (l != low_lane)}
 
-    def between(a, b, src, dst):
-        return Copy(l == a, l == b, (p, jnp.int32(b)), src, dst)
+    def between(a, b, src, dst, now=True):
+        return Copy(l == a, l == b, (p, jnp.int32(b)), src, dst, now)
 
     half = lanes // 2
     from_end = jnp.minimum(l, lanes - 1 - l)
@@ -222,13 +228,18 @@
         ]
         return ups, mids
 
-    def widen_finish(it, ups, mids):
+    def widen_corners(it, ups, mids, who):
         now = cur.at[it]
         for c, at in ((ups[1], 0), (ups[0], span - HALO)):
-            c.arrive()
+            pl.when(who & c.since)(c.copy.wait_recv)
             got = now.at[span + at : span + at + HALO]
-            mids.append(beside("before", got, now.at[2 * span + at : 2 * span + at + HALO]))
-            mids.append(beside("after", got, now.at[at : at + HALO]))
+            for side, plane in (("before", 2), ("after", 0)):
+                mids.append(Copy(
+                    who & has[side], who & has[opposite[side]], where[side],
+                    got, now.at[plane * span + at : plane * span + at + HALO],
+                ))
+
+    def widen_finish(ups, mids):
         for c in mids:
             c.arrive()
         departed.extend(ups + mids)
@@ -259,6 +270,10 @@
     for turn, k in enumerate(order):
         if turn == AHEAD % len(order):
             pass_on()
+        if turn == CORNERS % len(order):
+            widen_corners(0, ups, mids, from_end != half - 1)
+        if turn == FAR_CORNERS % len(order):
+            widen_corners(0, ups, mids, from_end == half - 1)
         to = (lax.rem(p + k, groups), l)
         direct = p >= 0
         for distance, offset in plan:
@@ -330,8 +345,17 @@
         for v in range(views):
             blurred[v * depth : (v + 1) * depth] = along_y(spread[v * depth : (v + 1) * depth], t_fwd[v])
 
-    widen_finish(0, ups, mids)
+    widen_finish(ups, mids)
     blur(0)
+
+    first = [
+        between(low_lane, far_low, passing.at[0, depth - HALO :], passing.at[1, 0:HALO], False),
+        between(high_lane, far_high, passing.at[0, 0:HALO], passing.at[1, 0:HALO], False),
+    ]
+    across = []
+    for c, a, b in ((first[0], far_low, high_lane), (first[1], far_high, low_lane)):
+        c.arrive()
+        across.append(between(a, b, passing.at[1, 0:HALO], beyond.at[1]))
 
     for always, sent, c in routes:
         if always is not None:
@@ -344,7 +368,9 @@
 
     for it in range(ITERS):
         if it > 0:
-            widen_finish(it, *widen_start(it))
+            ups, mids = widen_start(it)
+            widen_corners(it, ups, mids, p >= 0)
+            widen_finish(ups, mids)
             blur(it)
         y = iota((depth, width), 1)
         for v in range(views):
@@ -364,7 +390,7 @@
                 beside("before", mine.at[a:b], theirs.at[1, a:b]),
                 beside("after", mine.at[2 * span + a : 2 * span + b], theirs.at[0, a:b]),
             ])
-        edges, across = [], []
+        edges = []
         for n, (side, a) in enumerate((("up", 0), ("down", span - HALO))):
             for c in shares[n]:
                 c.arrive()
@@ -382,13 +408,8 @@
         correction = part[it, own] + (part_in[it, 0, mid] + part_in[it, 1, mid])
         if it + 1 < ITERS:
             passing[0] = correction
-            first = [
-                between(low_lane, far_low, passing.at[0, depth - HALO :], passing.at[1, 0:HALO]),
-                between(high_lane, far_high, passing.at[0, 0:HALO], passing.at[1, 0:HALO]),
-            ]
-            for c, a, b in ((first[0], far_low, high_lane), (first[1], far_high, low_lane)):
-                c.arrive()
-                across.append(between(a, b, passing.at[1, 0:HALO], beyond.at[1]))
+            for c in first:
+                c.start()
         for c in edges:
             c.arrive()
         rest = jnp.zeros((depth - HALO, width), F32)
@@ -436,7 +457,7 @@
     hbm = pl.BlockSpec(memory_space=pltpu.HBM)
     columns = -(-3 * span // 128) * 128
     plan, _ = relays(groups, lanes)
-    copies = 18 * ITERS + 6 + len(plan)
+    copies = 18 * ITERS + 10 + len(plan)
     vmem = lambda *shape: pltpu.VMEM(shape, F32)
     dma = lambda n: pltpu.SemaphoreType.DMA((n,))
     out = pl.pallas_call(

time: 108 us -> 105 us (0.972)
  the two profiles are of different devices: /device:TPU:127 before, /device:TPU:384 now
where the time goes in v4:
time: 105 us
  Pallas kernels  104 us (99%)
  local copies, waits for them, and re-layouts  1.57 us (1%)
    pallas_call x1, Pallas kernels, shards(): pl.pallas_call(functools.partial(kernel, groups, lanes, views, cap), out_...  104 us

profile of v4, /device:TPU:384, one launch (start us, length us, event | category | flops | bytes accessed | tf_op | source)
XLA Modules:
  0.0 105.3 jit_solution(14966614548630338869)
XLA Ops:
  0.0 103.7 %shard_map.73 = f32[32,1024]{1,0:T(8,128)} custom-call(f32[32,1024]{1,0:T(8,128)} %bitcast.6, f32[128,1024]{1,0:T(8,128)} %bitcast.4, s32[4,32]{1,0:T(4,128)} %bitcast.7, s32[4,32]{1,0:T(4,128)} %target_at.1, s32[4]{0:T(128)} %shift_at.1, f32[4,3]{1,0:T(4,128)} %psf_x_at.1, f32[4,2,41]{2,1,0:T(2,128)} %psf_yz_at.1), custom_call_target="tpu_custom_call" | custom-call | tf_op jit(solution)/shard_map/pallas_call | solution.py:463
  103.7 1.6 %copy.9 = f32[1,32,1024]{2,1,0:T(8,128)} copy(f32[1,32,1024]{2,1,0:T(8,128)} %bitcast.5) | data formatting | bytes 262144

commit v5 on v4

--- a/solution.py
+++ b/solution.py
@@ -8,8 +8,8 @@
 from jax.sharding import PartitionSpec as P
 
 ITERS = 2
-CORNERS = 9
-FAR_CORNERS = 12
+CORNERS = 3
+FAR_CORNERS = 14
 AHEAD = 1
 HALO = 24
 MESH = pl.DeviceIdType.MESH
@@ -173,13 +173,15 @@
     @pl.when(l == 0)
     def _():
         for it in range(ITERS):
-            cur[it, span : span + HALO] = jnp.zeros((HALO, width), F32)
+            for plane in range(3) if it == 0 else (1,):
+                cur[it, plane * span : plane * span + HALO] = jnp.zeros((HALO, width), F32)
             edge_in[it, 0] = jnp.zeros((HALO, width), F32)
 
     @pl.when(l == lanes - 1)
     def _():
         for it in range(ITERS):
-            cur[it, 2 * span - HALO : 2 * span] = jnp.zeros((HALO, width), F32)
+            for plane in range(3) if it == 0 else (1,):
+                cur[it, (plane + 1) * span - HALO : (plane + 1) * span] = jnp.zeros((HALO, width), F32)
             edge_in[it, 1] = jnp.zeros((HALO, width), F32)
 
     for c in loads:
@@ -228,16 +230,27 @@
         ]
         return ups, mids
 
-    def widen_corners(it, ups, mids, who):
+    def corners(it, c, at, who, mids):
         now = cur.at[it]
-        for c, at in ((ups[1], 0), (ups[0], span - HALO)):
-            pl.when(who & c.since)(c.copy.wait_recv)
-            got = now.at[span + at : span + at + HALO]
-            for side, plane in (("before", 2), ("after", 0)):
-                mids.append(Copy(
-                    who & has[side], who & has[opposite[side]], where[side],
-                    got, now.at[plane * span + at : plane * span + at + HALO],
-                ))
+        pl.when(who & c.since)(c.copy.wait_recv)
+        got = now.at[span + at : span + at + HALO]
+        for side, plane in (("before", 2), ("after", 0)):
+            mids.append(Copy(
+                who & has[side], who & has[opposite[side]], where[side],
+                got, now.at[plane * span + at : plane * span + at + HALO],
+            ))
+
+    def beside_planes(mids):
+        now = cur.at[0]
+        for c in mids:
+            c.arrive()
+        departed.extend(mids)
+        mids.clear()
+        for side, plane in (("before", 0), ("after", 2)):
+            lo, hi = plane * span, (plane + 1) * span
+            up, down = near["up"] & has[side], near["down"] & has[side]
+            mids.append(Copy(up, down, where["up"], now.at[lo + HALO : lo + 2 * HALO], now.at[hi - HALO : hi]))
+            mids.append(Copy(down, up, where["down"], now.at[hi - 2 * HALO : hi - HALO], now.at[lo : lo + HALO]))
 
     def widen_finish(ups, mids):
         for c in mids:
@@ -271,9 +284,10 @@
         if turn == AHEAD % len(order):
             pass_on()
         if turn == CORNERS % len(order):
-            widen_corners(0, ups, mids, from_end != half - 1)
+            beside_planes(mids)
         if turn == FAR_CORNERS % len(order):
-            widen_corners(0, ups, mids, from_end == half - 1)
+            corners(0, ups[1], 0, l == high_lane, mids)
+            corners(0, ups[0], span - HALO, l == low_lane, mids)
         to = (lax.rem(p + k, groups), l)
         direct = p >= 0
         for distance, offset in plan:
@@ -345,6 +359,8 @@
         for v in range(views):
             blurred[v * depth : (v + 1) * depth] = along_y(spread[v * depth : (v + 1) * depth], t_fwd[v])
 
+    pl.when(ups[1].since & (l != high_lane))(ups[1].copy.wait_recv)
+    pl.when(ups[0].since & (l != low_lane))(ups[0].copy.wait_recv)
     widen_finish(ups, mids)
     blur(0)
 
@@ -369,7 +385,8 @@
     for it in range(ITERS):
         if it > 0:
             ups, mids = widen_start(it)
-            widen_corners(it, ups, mids, p >= 0)
+            for c, at in ((ups[1], 0), (ups[0], span - HALO)):
+                corners(it, c, at, p >= 0, mids)
             widen_finish(ups, mids)
             blur(it)
         y = iota((depth, width), 1)
@@ -457,7 +474,7 @@
     hbm = pl.BlockSpec(memory_space=pltpu.HBM)
     columns = -(-3 * span // 128) * 128
     plan, _ = relays(groups, lanes)
-    copies = 18 * ITERS + 10 + len(plan)
+    copies = 18 * ITERS + 14 + len(plan)
     vmem = lambda *shape: pltpu.VMEM(shape, F32)
     dma = lambda n: pltpu.SemaphoreType.DMA((n,))
     out = pl.pallas_call(

time: 105 us -> 105 us (level)
  the two profiles are of different devices: /device:TPU:384 before, /device:TPU:223 now
where the time goes in v5:
time: 105 us
  Pallas kernels  103 us (98%)
  local copies, waits for them, and re-layouts  1.57 us (1%)
    pallas_call x1, Pallas kernels, shards(): pl.pallas_call(functools.partial(kernel, groups, lanes, views, cap), out_...  103 us

profile of v5, /device:TPU:223, one launch (start us, length us, event | category | flops | bytes accessed | tf_op | source)
XLA Modules:
  0.0 104.6 jit_solution(12806099764996958482)
XLA Ops:
  0.0 103.0 %shard_map.73 = f32[32,1024]{1,0:T(8,128)} custom-call(f32[32,1024]{1,0:T(8,128)} %bitcast.6, f32[128,1024]{1,0:T(8,128)} %bitcast.4, s32[4,32]{1,0:T(4,128)} %bitcast.7, s32[4,32]{1,0:T(4,128)} %target_at.1, s32[4]{0:T(128)} %shift_at.1, f32[4,3]{1,0:T(4,128)} %psf_x_at.1, f32[4,2,41]{2,1,0:T(2,128)} %psf_yz_at.1), custom_call_target="tpu_custom_call" | custom-call | tf_op jit(solution)/shard_map/pallas_call | solution.py:480
  103.0 1.6 %copy.9 = f32[1,32,1024]{2,1,0:T(8,128)} copy(f32[1,32,1024]{2,1,0:T(8,128)} %bitcast.5) | data formatting | bytes 262144
